TPU v7x, 256 devices: a whole 4x4x8 slice. The times are simulated.
256 devices in a mesh: dp: 32 (over x, z), tensor: 8 (over y, core).
Axes of the slice: x: 4, y: 4, z: 8, core: 2. Of those that a mesh axis runs over, the one named last changes fastest.
Arguments:
- decoder_states: bfloat16 [1024, 16, 4096], P(('dp', 'tensor')), may hold values from -24 to 24
- encoder_memory: bfloat16 [1024, 4, 4096], P('dp', None, 'tensor'), may hold values from -6 to 6
- memory_route: int32 [1024], replicated, may hold values from 0 to 1023, as said below
- memory_length: int32 [1024], replicated, may hold values from 1 to 4
- target_length: int32 [1024], P(('dp', 'tensor')), may hold values from 1 to 16
- objective: int32 [1024], P(('dp', 'tensor')), may hold values from 0 to 2
- mode_table: bfloat16 [3, 4096], replicated, may hold values from -6 to 6
- norm_gain: bfloat16 [4096], replicated, may hold values from 0.5 to 1.5
- w_query: bfloat16 [4096, 2048], P(None, 'tensor'), may hold values from -0.09375 to 0.09375
- w_key: bfloat16 [4096, 2048], P(None, 'tensor'), may hold values from -0.09375 to 0.09375
- w_value: bfloat16 [4096, 2048], P(None, 'tensor'), may hold values from -0.09375 to 0.09375
- w_output: bfloat16 [2048, 4096], P('tensor'), may hold values from -0.125 to 0.125
- cotangent: bfloat16 [1024, 16, 4096], P(('dp', 'tensor')), may hold values from -24 to 24
Outputs:
- layer_output: bfloat16 [1024, 16, 4096], P(('dp', 'tensor'))
- grad_decoder: bfloat16 [1024, 16, 4096], P(('dp', 'tensor'))
- grad_memory: bfloat16 [1024, 4, 4096], P('dp', None, 'tensor')
- grad_query: bfloat16 [4096, 2048], P('dp', 'tensor')
- grad_key: bfloat16 [4096, 2048], P('dp', 'tensor')
- grad_value: bfloat16 [4096, 2048], P('dp', 'tensor')
- grad_output: bfloat16 [2048, 4096], P('tensor', 'dp')
- grad_gain: float32 [4096], replicated
- grad_mode: float32 [3, 4096], replicated
Inputs may be any that keep to these rules, and one draw needn't show every extreme that they name: `memory_route`: A permutation of the slots. Slot s belongs to decoder owner s // 32; the examples e with e // 32 equal to one encoder owner send exactly 1 examples to every decoder owner.
All inputs are finite; a program needn't handle non-finite values.
Results may differ from a plain program's by a relative error of at most 0.022.
Values may be sent and summed in bfloat16 or wider, within the bound.
A program may use at most 128 MiB of HBM per device.

v0:
```python
import jax
import jax.numpy as jnp
from jax import lax
from jax.sharding import PartitionSpec as P

HD = 256


def soft_weights(query_heads, key_heads, valid_keys, score_scale):
    scores = (
        jnp.einsum("bthd,bjhd->bhtj", query_heads, key_heads, preferred_element_type=jnp.float32)
        * score_scale
    )
    scores = jnp.where(valid_keys[:, None, None, :], scores, -1e30)
    row_max = jnp.max(scores, axis=-1, keepdims=True)
    expo = jnp.exp(scores - row_max)
    return expo / jnp.sum(expo, axis=-1, keepdims=True)


def shards(
    decoder_states,
    encoder_memory,
    memory_route,
    memory_length,
    target_length,
    objective,
    mode_table,
    norm_gain,
    w_query,
    w_key,
    w_value,
    w_output,
    cotangent,
):
    local_ex, dec_rows, model_width = decoder_states.shape
    group_ex, mem_rows, col_width = encoder_memory.shape
    head_width = w_query.shape[1]
    head_count = head_width // HD
    peer_count = lax.axis_size("dp")
    per_pair = group_ex // peer_count
    score_scale = HD ** (-0.5)
    my_owner = lax.axis_index("dp")
    objective_hot = (objective[:, None] == jnp.arange(3)[None, :]).astype(jnp.float32)
    mode_rows = jnp.dot(
        objective_hot, mode_table.astype(jnp.float32), precision=lax.Precision.HIGHEST
    )
    shifted = decoder_states.astype(jnp.float32) + mode_rows[:, None, :]
    inv_rms = lax.rsqrt(jnp.mean(shifted * shifted, axis=-1, keepdims=True) + 1e-06)
    normed = shifted * inv_rms
    gain_wide = norm_gain.astype(jnp.float32)
    normed_in = (normed * gain_wide).astype(jnp.bfloat16)
    all_normed = lax.all_gather(normed_in, "tensor", axis=0, tiled=True)
    own_route = lax.dynamic_slice_in_dim(memory_route, my_owner * group_ex, group_ex, 0)
    send_order = jnp.argsort(own_route)
    send_rows = encoder_memory[send_order].reshape(peer_count, per_pair, mem_rows, col_width)
    inverse_route = jnp.argsort(memory_route)
    arriving = lax.dynamic_slice_in_dim(inverse_route, my_owner * group_ex, group_ex, 0)
    arrive_source = arriving // group_ex
    slot_index = jnp.arange(group_ex)
    earlier = (arrive_source[None, :] == arrive_source[:, None]) & (
        slot_index[None, :] < slot_index[:, None]
    )
    arrive_rank = jnp.sum(earlier.astype(jnp.int32), axis=1)
    flat_index = arrive_source * per_pair + arrive_rank
    key_length = memory_length[arriving]
    queries = jnp.dot(all_normed, w_query, preferred_element_type=jnp.float32).astype(jnp.bfloat16)
    received = lax.all_to_all(send_rows, "dp", split_axis=0, concat_axis=0, tiled=True)
    memory_part = received.reshape(group_ex, mem_rows, col_width)[flat_index]
    memory_full = lax.all_gather(memory_part, "tensor", axis=2, tiled=True)
    key_rows = jnp.dot(memory_full, w_key, preferred_element_type=jnp.float32).astype(jnp.bfloat16)
    value_rows = jnp.dot(memory_full, w_value, preferred_element_type=jnp.float32).astype(
        jnp.bfloat16
    )
    query_heads = queries.reshape(group_ex, dec_rows, head_count, HD)
    key_heads = key_rows.reshape(group_ex, mem_rows, head_count, HD)
    value_heads = value_rows.reshape(group_ex, mem_rows, head_count, HD)
    valid_keys = jnp.arange(mem_rows)[None, :] < key_length[:, None]
    probabilities = soft_weights(query_heads, key_heads, valid_keys, score_scale)
    probs_low = probabilities.astype(jnp.bfloat16)
    context = jnp.einsum(
        "bhtj,bjhd->bthd", probs_low, value_heads, preferred_element_type=jnp.float32
    ).astype(jnp.bfloat16)
    context = context.reshape(group_ex, dec_rows, head_width)
    rows_in = context
    attended = lax.psum_scatter(
        jnp.dot(rows_in, w_output, preferred_element_type=jnp.float32).astype(jnp.bfloat16),
        "tensor",
        scatter_dimension=0,
        tiled=True,
    ).astype(jnp.float32)
    layer_output = (shifted + attended).astype(jnp.bfloat16)
    live_rows = jnp.arange(dec_rows)[None, :] < target_length[:, None]
    masked_cot = jnp.where(live_rows[:, :, None], cotangent, jnp.zeros_like(cotangent))
    all_cot = lax.all_gather(masked_cot, "tensor", axis=0, tiled=True)
    grad_context = jnp.einsum(
        "btd,wd->btw", all_cot, w_output, preferred_element_type=jnp.float32
    ).astype(jnp.bfloat16)
    output_weight_term = jnp.einsum(
        "btw,btd->wd", context, all_cot, preferred_element_type=jnp.float32
    )
    grad_output = lax.psum_scatter(
        output_weight_term.astype(jnp.bfloat16), "dp", scatter_dimension=1, tiled=True
    )
    grad_ctx_heads = grad_context.reshape(group_ex, dec_rows, head_count, HD)
    grad_probs = jnp.einsum(
        "bthd,bjhd->bhtj", grad_ctx_heads, value_heads, preferred_element_type=jnp.float32
    )
    grad_scores = (
        probabilities
        * (grad_probs - jnp.sum(probabilities * grad_probs, axis=-1, keepdims=True))
        * score_scale
    ).astype(jnp.bfloat16)
    grad_q = jnp.einsum(
        "bhtj,bjhd->bthd", grad_scores, key_heads, preferred_element_type=jnp.float32
    ).astype(jnp.bfloat16)
    grad_q = grad_q.reshape(group_ex, dec_rows, head_width)
    grad_k = jnp.einsum(
        "bhtj,bthd->bjhd", grad_scores, query_heads, preferred_element_type=jnp.float32
    ).astype(jnp.bfloat16)
    grad_k = grad_k.reshape(group_ex, mem_rows, head_width)
    grad_v = jnp.einsum(
        "bhtj,bthd->bjhd", probs_low, grad_ctx_heads, preferred_element_type=jnp.float32
    ).astype(jnp.bfloat16)
    grad_v = grad_v.reshape(group_ex, mem_rows, head_width)
    unsort = jnp.argsort(send_order)
    back_order = jnp.argsort(flat_index)
    memory_term = jnp.einsum("bjw,dw->bjd", grad_k, w_key, preferred_element_type=jnp.float32)
    memory_term = memory_term + jnp.einsum(
        "bjw,dw->bjd", grad_v, w_value, preferred_element_type=jnp.float32
    )
    grad_part = lax.psum_scatter(
        memory_term.astype(jnp.bfloat16), "tensor", scatter_dimension=2, tiled=True
    )
    back_rows = grad_part[back_order].reshape(peer_count, per_pair, mem_rows, col_width)
    returned = lax.all_to_all(back_rows, "dp", split_axis=0, concat_axis=0, tiled=True)
    grad_memory = returned.reshape(group_ex, mem_rows, col_width)[unsort]
    weight_terms = (
        jnp.einsum("btd,btw->dw", all_normed, grad_q, preferred_element_type=jnp.float32),
        jnp.einsum("bjd,bjw->dw", memory_full, grad_k, preferred_element_type=jnp.float32),
        jnp.einsum("bjd,bjw->dw", memory_full, grad_v, preferred_element_type=jnp.float32),
    )
    summed_query, summed_key, summed_value = (
        lax.psum_scatter(
            weight_terms[0].astype(jnp.bfloat16), "dp", scatter_dimension=0, tiled=True
        ).astype(jnp.float32),
        lax.psum_scatter(
            weight_terms[1].astype(jnp.bfloat16), "dp", scatter_dimension=0, tiled=True
        ).astype(jnp.float32),
        lax.psum_scatter(
            weight_terms[2].astype(jnp.bfloat16), "dp", scatter_dimension=0, tiled=True
        ).astype(jnp.float32),
    )
    grad_query = summed_query.astype(jnp.bfloat16)
    grad_key = summed_key.astype(jnp.bfloat16)
    grad_value = summed_value.astype(jnp.bfloat16)
    rows_in = grad_q
    grad_normed = lax.psum_scatter(
        jnp.einsum("btw,dw->btd", rows_in, w_query, preferred_element_type=jnp.float32).astype(
            jnp.bfloat16
        ),
        "tensor",
        scatter_dimension=0,
        tiled=True,
    ).astype(jnp.float32)
    scaled = gain_wide * grad_normed
    dot_mean = jnp.mean(scaled * normed, axis=-1, keepdims=True)
    grad_shift = masked_cot.astype(jnp.float32) + inv_rms * (scaled - normed * dot_mean)
    grad_decoder = grad_shift.astype(jnp.bfloat16)
    gain_term = jnp.sum(grad_normed * normed, axis=(0, 1))
    mode_term = jnp.dot(
        objective_hot.T, jnp.sum(grad_shift, axis=1), precision=lax.Precision.HIGHEST
    )
    grad_gain, grad_mode = lax.psum((gain_term, mode_term), ("dp", "tensor"))
    return (
        layer_output,
        grad_decoder,
        grad_memory,
        grad_query,
        grad_key,
        grad_value,
        grad_output,
        grad_gain,
        grad_mode,
    )


def solution(mesh):
    return jax.shard_map(
        shards,
        mesh=mesh,
        in_specs=(
            P(("dp", "tensor"), None, None),
            P("dp", None, "tensor"),
            P(),
            P(),
            P(("dp", "tensor")),
            P(("dp", "tensor")),
            P(),
            P(),
            P(None, "tensor"),
            P(None, "tensor"),
            P(None, "tensor"),
            P("tensor", None),
            P(("dp", "tensor"), None, None),
        ),
        out_specs=(
            P(("dp", "tensor"), None, None),
            P(("dp", "tensor"), None, None),
            P("dp", None, "tensor"),
            P("dp", "tensor"),
            P("dp", "tensor"),
            P("dp", "tensor"),
            P("tensor", "dp"),
            P(),
            P(),
        ),
        check_vma=False,
    )
```

profile of v0, /device:TPU:1, one launch (start us, length us, event | category | flops | bytes accessed | tf_op | source)
XLA Modules:
  0.0 1396.5 jit_solution(832681052699594981)
XLA Ops:
  7.2 0.9 dynamic_slice.6
  8.1 1.6 sort.62
  9.8 2.2 gather_fusion
  12.0 11.9 all-to-all-start
  23.9 5.1 sort.63
  29.8 3.2 all-to-all-done
  35.2 1.0 fusion.71
  36.1 1.3 multiply_reduce_fusion
  37.4 1.0 multiply_convert_fusion
  40.3 19.1 %all-gather.9.cloned.1.call-done = bf16[32,4,4096]{2,0,1:T(8,128)(2,1)} async-done(((bf16[32,4,512]{2,0,1:T(8,128)(2,1)}), bf16[32,4,4096]{2,0,1:T(8,128)(2,1)}) %all-gather.9.cloned.1.call-update) | async-done | bytes 1048592 | tf_op jit(solution)/shard_map/all_gather | solution.py:69
  59.5 2.5 fusion.33
  62.8 33.7 %all-gather.5.cloned.1.call-done = bf16[32,16,4096]{2,1,0:T(8,128)(2,1)} async-done(((bf16[4,16,4096]{2,1,0:T(8,128)(2,1)}), bf16[32,16,4096]{2,1,0:T(8,128)(2,1)}) %all-gather.5.cloned.1.call-update) | async-done | bytes 4194320 | tf_op jit(solution)/shard_map/all_gather | solution.py:52
  96.5 3.4 fusion.22
  100.8 32.8 %all-gather.7.cloned.1.call-done = bf16[32,16,4096]{2,1,0:T(8,128)(2,1)} async-done(((bf16[4,16,4096]{2,1,0:T(8,128)(2,1)}), bf16[32,16,4096]{2,1,0:T(8,128)(2,1)}) %all-gather.7.cloned.1.call-update) | async-done | bytes 4194320 | tf_op jit(solution)/shard_map/all_gather | solution.py:94
  133.6 4.9 fusion.25
  138.5 1.1 fusion.38
  139.6 1.1 fusion.60
  140.8 1.2 fusion.37
  142.0 2.6 fusion.10
  144.6 1.8 fusion.6
  146.5 1.3 fusion.29
  147.8 3.2 convolution_convert_fusion
  151.1 1.2 fusion.28
  152.3 4.8 convolution_convert_fusion.1
  157.2 4.8 fusion.5
  162.1 4.1 copy.71
  167.1 4.8 fusion.4
  172.8 2.1 fusion.2
  175.7 2.0 fusion.3
  178.4 1.6 sort.65
  180.0 1.6 sort.64
  181.6 1.0 copy.67
  182.6 1.3 gather_fusion.3
  184.0 9.6 all-to-all-start.1
  193.6 26.1 %reduce-scatter.12.cloned.1.call-done = bf16[4,16,4096]{2,1,0:T(8,128)(2,1)} async-done(((bf16[32,16,4096]{2,1,0:T(8,128)(2,1)}), bf16[4,16,4096]{2,1,0:T(8,128)(2,1)}) %reduce-scatter.12.cloned.1.call-update) | async-done | bytes 524304 | tf_op jit(solution)/shard_map/reduce_scatter | solution.py:157
  219.6 1.4 fusion.45
  221.1 40.0 %reduce-scatter.10.cloned.1.call-done = bf16[4,16,4096]{2,1,0:T(8,128)(2,1)} async-done(((bf16[32,16,4096]{2,1,0:T(8,128)(2,1)}), bf16[4,16,4096]{2,1,0:T(8,128)(2,1)}) %reduce-scatter.10.cloned.1.call-update) | async-done | bytes 524304 | tf_op jit(solution)/shard_map/reduce_scatter | solution.py:85
  261.1 3.4 fusion.50
  264.4 0.9 fusion.70
  265.4 1.3 gather_fusion.4
  266.8 211.1 %reduce-scatter.22.cloned.1.call-done = bf16[128,256]{1,0:T(8,128)(2,1)} async-done(((bf16[4096,256]{1,0:T(8,128)(2,1)}), bf16[128,256]{1,0:T(8,128)(2,1)}) %reduce-scatter.22.cloned.1.call-update) | async-done | bytes 65552
  477.9 1.6 copy.72
  479.4 217.9 %reduce-scatter.16.cloned.1.call-done = bf16[128,256]{1,0:T(8,128)(2,1)} async-done(((bf16[4096,256]{1,0:T(8,128)(2,1)}), bf16[128,256]{1,0:T(8,128)(2,1)}) %reduce-scatter.16.cloned.1.call-update) | async-done | bytes 65552 | tf_op jit(solution)/shard_map/reduce_scatter | solution.py:143
  697.3 219.1 %reduce-scatter.18.cloned.1.call-done = bf16[128,256]{1,0:T(8,128)(2,1)} async-done(((bf16[4096,256]{1,0:T(8,128)(2,1)}), bf16[128,256]{1,0:T(8,128)(2,1)}) %reduce-scatter.18.cloned.1.call-update) | async-done | bytes 65552 | tf_op jit(solution)/shard_map/reduce_scatter | solution.py:146
  916.4 219.3 %reduce-scatter.20.cloned.1.call-done = bf16[128,256]{1,0:T(8,128)(2,1)} async-done(((bf16[4096,256]{1,0:T(8,128)(2,1)}), bf16[128,256]{1,0:T(8,128)(2,1)}) %reduce-scatter.20.cloned.1.call-update) | async-done | bytes 65552 | tf_op jit(solution)/shard_map/reduce_scatter | solution.py:149
  1135.7 251.5 %all-reduce.3.cloned.1.call-done = (f32[4096]{0:T(1024)}, f32[3,4096]{1,0:T(4,128)}) async-done(((f32[4096]{0:T(1024)}, f32[3,4096]{1,0:T(4,128)}), (f32[4096]{0:T(1024)}, f32[3,4096]{1,0:T(4,128)})) %all-reduce.3.cloned.1.call-update) | async-done | bytes 65552 | tf_op jit(solution)/shard_map/psum | solution.py:173
  1387.2 1.3 copy.91
  1388.5 1.5 copy.92
  (111 shorter events, 10.0 us)
Async XLA Ops:
  7.2 89.3 %copy-start = (bf16[4096,256]{1,0:T(8,128)(2,1)S(1)}, bf16[4096,256]{1,0:T(8,128)(2,1)}, u32[]{:S(2)}) copy-start(bf16[4096,256]{1,0:T(8,128)(2,1)} %param.21) | copy-start | bytes 6291460
  7.2 30.2 %copy-start.5 = (bf16[4,16,4096]{2,1,0:T(8,128)(2,1)S(1)}, bf16[4,16,4096]{2,1,0:T(8,128)(2,1)}, u32[]{:S(2)}) copy-start(bf16[4,16,4096]{2,1,0:T(8,128)(2,1)} %param.13) | copy-start | bytes 1572868
  7.2 31.3 %copy-start.22 = (s32[4]{0:T(128)S(1)}, s32[4]{0:T(128)}, u32[]{:S(2)}) copy-start(s32[4]{0:T(128)} %param.17) | copy-start | bytes 52
  7.2 31.3 %copy-start.7 = (bf16[4,16,4096]{2,1,0:T(8,128)(2,1)S(1)}, bf16[4,16,4096]{2,1,0:T(8,128)(2,1)}, u32[]{:S(2)}) copy-start(bf16[4,16,4096]{2,1,0:T(8,128)(2,1)} %param.25) | copy-start | bytes 1572868
  9.8 2.2 copy-start.24
  12.0 21.0 %all-to-all-start = ((bf16[32,1,4,512]{3,2,1,0:T(4,128)(2,1)}), bf16[32,1,4,512]{3,2,1,0:T(4,128)(2,1)S(1)}, u32[]{:S(2)}, u32[]{:S(2)}) async-start(bf16[32,1,4,512]{3,2,1,0:T(4,128)(2,1)} %bitcast), calls=%async_computation | async-start | bytes 262144 | tf_op jit(solution)/shard_map/all_to_all | solution.py:67
  23.9 35.6 %all-gather.9.cloned.1.call-start = ((), (), s32[]{:S(2)}) async-start(), calls=%async_computation.17 | async-start | bytes 1179648 | tf_op jit(solution)/shard_map/all_gather | solution.py:69
  34.4 5.2 copy-start.1
  34.4 62.1 %all-gather.5.cloned.1.call-start = ((), (), s32[]{:S(2)}) async-start(), calls=%async_computation.9 | async-start | bytes 4718592 | tf_op jit(solution)/shard_map/all_gather | solution.py:52
  37.4 2.9 copy-start.16
  38.4 95.2 %all-gather.7.cloned.1.call-start = ((), (), s32[]{:S(2)}) async-start(), calls=%async_computation.11 | async-start | bytes 4718592 | tf_op jit(solution)/shard_map/all_gather | solution.py:94
  38.6 1.0 copy-start.19
  39.5 142.1 %reduce-scatter.14.cloned.1.call-start = ((), (), s32[]{:S(2)}) async-start(), calls=%async_computation.13 | async-start | bytes 1179648 | tf_op jit(solution)/shard_map/reduce_scatter | solution.py:131
  59.5 2.5 copy-start.2
  59.5 2.9 copy-start.3
  62.3 37.6 %copy-start.11 = (bf16[32,4,256]{2,0,1:T(8,128)(2,1)}, bf16[32,4,256]{2,0,1:T(8,128)(2,1)S(1)}, u32[]{:S(2)}) copy-start(bf16[32,4,256]{2,0,1:T(8,128)(2,1)S(1)} %fusion.33) | copy-start | bytes 196612
  99.9 0.7 copy-start.26
  100.6 37.8 %copy-start.27 = (f32[32,16,4]{1,2,0:T(4,128)}, f32[32,16,4]{1,2,0:T(4,128)S(1)}, u32[]{:S(2)}) copy-start(f32[32,16,4]{1,2,0:T(4,128)S(1)} %fusion.43) | copy-start | bytes 24580
  100.7 37.7 %copy-start.29 = (f32[32,16]{1,0:T(8,128)}, f32[32,16]{1,0:T(8,128)S(1)}, u32[]{:S(2)}) copy-start(f32[32,16]{1,0:T(8,128)S(1)} %get-tuple-element.36) | copy-start | bytes 6148
  100.8 40.0 %copy-start.28 = (f32[32,16,4]{1,2,0:T(4,128)}, f32[32,16,4]{1,2,0:T(4,128)S(1)}, u32[]{:S(2)}) copy-start(f32[32,16,4]{1,2,0:T(4,128)S(1)} %get-tuple-element.37) | copy-start | bytes 24580
  139.6 5.0 copy-start.14
  140.8 3.8 copy-start.23
  142.0 2.6 copy-start.12
  142.0 2.6 copy-start.4
  146.5 73.2 %reduce-scatter.12.cloned.1.call-start = ((), (), s32[]{:S(2)}) async-start(), calls=%async_computation.12 | async-start | bytes 4718592 | tf_op jit(solution)/shard_map/reduce_scatter | solution.py:157
  147.8 3.2 copy-start.9
  151.1 110.0 %reduce-scatter.10.cloned.1.call-start = ((), (), s32[]{:S(2)}) async-start(), calls=%async_computation.10 | async-start | bytes 4718592 | tf_op jit(solution)/shard_map/reduce_scatter | solution.py:85
  157.2 320.7 %reduce-scatter.22.cloned.1.call-start = ((), (), s32[]{:S(2)}) async-start(), calls=%async_computation.18 | async-start | bytes 2162688
  166.2 1.0 copy-start.10
  166.2 531.1 %reduce-scatter.16.cloned.1.call-start = ((), (), s32[]{:S(2)}) async-start(), calls=%async_computation.14 | async-start | bytes 2162688 | tf_op jit(solution)/shard_map/reduce_scatter | solution.py:143
  171.9 0.8 copy-start.13
  172.0 744.4 %reduce-scatter.18.cloned.1.call-start = ((), (), s32[]{:S(2)}) async-start(), calls=%async_computation.15 | async-start | bytes 2162688 | tf_op jit(solution)/shard_map/reduce_scatter | solution.py:146
  174.9 0.8 copy-start.15
  174.9 960.8 %reduce-scatter.20.cloned.1.call-start = ((), (), s32[]{:S(2)}) async-start(), calls=%async_computation.16 | async-start | bytes 2162688 | tf_op jit(solution)/shard_map/reduce_scatter | solution.py:149
  177.8 0.6 copy-start.25
  177.8 2.2 copy-start.21
  177.8 41.8 %copy-start.6 = (bf16[4,16,4096]{2,1,0:T(8,128)(2,1)S(1)}, bf16[4,16,4096]{2,1,0:T(8,128)(2,1)}, u32[]{:S(2)}) copy-start(bf16[4,16,4096]{2,1,0:T(8,128)(2,1)} %param.13) | copy-start | bytes 1572868
  177.8 41.8 %copy-start.17 = (f32[4,16]{1,0:T(4,128)S(1)}, f32[4,16]{1,0:T(4,128)}, u32[]{:S(2)}) copy-start(f32[4,16]{1,0:T(4,128)} %copy-done.16) | copy-start | bytes 772
  177.8 83.3 %copy-start.8 = (bf16[4,16,4096]{2,1,0:T(8,128)(2,1)S(1)}, bf16[4,16,4096]{2,1,0:T(8,128)(2,1)}, u32[]{:S(2)}) copy-start(bf16[4,16,4096]{2,1,0:T(8,128)(2,1)} %param.25) | copy-start | bytes 1572868
  177.8 83.2 %copy-start.20 = (pred[4,16]{1,0:T(4,128)(4,1)S(1)}, pred[4,16]{1,0:T(4,128)(4,1)}, u32[]{:S(2)}) copy-start(pred[4,16]{1,0:T(4,128)(4,1)} %copy-done.19) | copy-start | bytes 196
  184.0 81.5 %all-to-all-start.1 = ((bf16[32,1,4,512]{3,2,1,0:T(4,128)(2,1)}), bf16[32,1,4,512]{3,2,1,0:T(4,128)(2,1)S(1)}, u32[]{:S(2)}, u32[]{:S(2)}) async-start(bf16[32,1,4,512]{3,2,1,0:T(4,128)(2,1)} %bitcast.19), calls=%async_computation.4 | async-start | bytes 262144 | tf_op jit(solution)/shard_map/all_to_all | solution.py:135
  193.5 70.9 %copy-start.18 = (s32[4]{0:T(128)S(1)}, s32[4]{0:T(128)}, u32[]{:S(2)}) copy-start(s32[4]{0:T(128)} %param.18) | copy-start | bytes 52
  193.5 1193.6 %all-reduce.3.cloned.1.call-start = ((), (), s32[]{:S(2)}) async-start(), calls=%async_computation.19 | async-start | bytes 163840 | tf_op jit(solution)/shard_map/psum | solution.py:173
Sparse Core Ops, SparseCore 0:
  34.5 24.9 all-gather.8
  61.9 34.5 all-gather.4
  98.9 34.6 all-gather.6
  146.6 31.5 reduce-scatter.13
  180.6 39.0 reduce-scatter.11
  222.0 38.9 reduce-scatter.9
  264.9 212.9 reduce-scatter.21
  482.8 214.5 reduce-scatter.15
  701.7 214.6 reduce-scatter.17
  921.1 214.5 reduce-scatter.19
  1142.5 244.6 all-reduce.2
where the time goes:
time: 1400 us
  waiting for transfers between devices  1270 us (91%)
  matrix products  45.6 us (3%)
  starting transfers between devices  22.1 us (2%)
  local copies, waits for them, and re-layouts  21 us (2%)
  other arithmetic  19.6 us (1%)
  between operations  14.3 us (1%)
    psum x1, waiting for transfers between devices, shards(): grad_gain, grad_mode = lax.psum((gain_term, mode_term), ('dp', 'tensor'))  251 us
    reduce_scatter x1, waiting for transfers between devices, shards(): lax.psum_scatter(weight_terms[2].astype(jnp.bfloat16), 'dp', scatter_dime...  219 us
    reduce_scatter x1, waiting for transfers between devices, shards(): lax.psum_scatter(weight_terms[1].astype(jnp.bfloat16), 'dp', scatter_dime...  219 us
    reduce_scatter x1, waiting for transfers between devices, shards(): lax.psum_scatter(weight_terms[0].astype(jnp.bfloat16), 'dp', scatter_dime...  218 us
    unnamed x12, waiting for transfers between devices  211 us
    reduce_scatter x1, waiting for transfers between devices, shards(): lax.psum_scatter(jnp.dot(rows_in, w_output, preferred_element_type=jnp.fl...  40 us
    all_gather x1, waiting for transfers between devices, shards(): all_normed = lax.all_gather(normed_in, 'tensor', axis=0, tiled=True)  33.7 us
    all_gather x1, waiting for transfers between devices, shards(): all_cot = lax.all_gather(masked_cot, 'tensor', axis=0, tiled=True)  32.8 us
  transfers between devices with their start and end apart: 13, of which 11 were waited for; matrix products, arithmetic and copies ran while one was open for 4% of the time, Pallas kernels for 0%

commit v1 on v0

v1 whole, which is shorter than its diff:
```python
import jax
import jax.numpy as jnp
from jax import lax
from jax.experimental import pallas as pl
from jax.experimental.pallas import tpu as pltpu
from jax.sharding import PartitionSpec as P

HD = 256
D = 4096
NX, NZ, NY = 4, 8, 4
NDP, NT = 32, 8
NSEM = 320
BF = jnp.bfloat16
F32 = jnp.float32
MESH = pl.DeviceIdType.MESH
NT_DIMS = (((1,), (1,)), ((), ()))

SCRATCH = {
    "wq": ((D, HD), BF),
    "wk": ((D, HD), BF),
    "wv": ((D, HD), BF),
    "wo": ((HD, D), BF),
    "nall": ((8, 64, D), BF),
    "call": ((8, 64, D), BF),
    "mall": ((8, 128, 512), BF),
    "a_out": ((32, 16, 128), BF),
    "a_in": ((32, 16, 128), BF),
    "b_out": ((32, 16, 128), BF),
    "b_in": ((32, 16, 128), BF),
    "shifted": ((64, D), F32),
    "inv": ((64, 128), F32),
    "q": ((512, HD), BF),
    "k": ((128, HD), BF),
    "v": ((128, HD), BF),
    "ctx": ((8, 64, HD), BF),
    "gctx": ((512, HD), BF),
    "gq": ((8, 64, HD), BF),
    "gk": ((128, HD), BF),
    "gv": ((128, HD), BF),
    "ctx_t": ((HD, 512), BF),
    "gq_t": ((HD, 512), BF),
    "gk_t": ((HD, 128), BF),
    "gv_t": ((HD, 128), BF),
    "p": ((512, 128), F32),
    "sib_out": ((4, 64, D), BF),
    "sib_in": ((4, 64, D), BF),
    "att": ((4, 64, D), BF),
    "att_r": ((2, 64, D), BF),
    "att_l": ((2, 64, D), BF),
    "gn": ((4, 64, D), BF),
    "gn_r": ((2, 64, D), BF),
    "gn_l": ((2, 64, D), BF),
    "msib_out": ((4, 128, 512), BF),
    "msib_in": ((4, 128, 512), BF),
    "mt": ((4, 128, 512), BF),
    "mt_r": ((2, 128, 512), BF),
    "mt_l": ((2, 128, 512), BF),
    "part": ((4, 8, D), F32),
    "s_out": ((8, 8, 256), F32),
    "s_in": ((8, 8, 256), F32),
    "s_x": ((4, 8, 256), F32),
    "s_z": ((8, 8, 256), F32),
    "s_all": ((8, 8, 256), F32),
}
for _name in ("tv", "tq"):
    SCRATCH[_name] = ((8, 1024, 128), BF)
    SCRATCH[_name + "_r"] = ((4, 1024, 128), BF)
    SCRATCH[_name + "_l"] = ((4, 1024, 128), BF)
    SCRATCH[_name + "2"] = ((4, 256, 128), BF)
    SCRATCH[_name + "2_r"] = ((2, 256, 128), BF)
    SCRATCH[_name + "2_l"] = ((2, 256, 128), BF)
for _name in ("to", "tk"):
    SCRATCH[_name] = ((4, 2048, 128), BF)
    SCRATCH[_name + "_r"] = ((2, 2048, 128), BF)
    SCRATCH[_name + "_l"] = ((2, 2048, 128), BF)
    SCRATCH[_name + "2"] = ((8, 256, 128), BF)
    SCRATCH[_name + "2_r"] = ((4, 256, 128), BF)
    SCRATCH[_name + "2_l"] = ((4, 256, 128), BF)


class Links:
    def __init__(self, send, recv):
        self.send, self.recv, self.used, self.started = send, recv, 0, []

    def take(self, count):
        first = self.used
        self.used += count
        assert self.used <= NSEM
        return first

    def at(self, src, dst, index, peer):
        return pltpu.make_async_remote_copy(
            src_ref=src,
            dst_ref=dst,
            send_sem=self.send.at[index],
            recv_sem=self.recv.at[index],
            device_id=peer,
            device_id_type=MESH,
        )

    def copy(self, src, dst, peer):
        return self.at(src, dst, self.take(1), peer)

    def start(self, *copies):
        for one in copies:
            one.start()
            self.started.append(one)

    def finish_sends(self):
        for one in self.started:
            one.wait_send()
        self.started = []


def rows_loop(total, step, body):
    @pl.loop(0, total // step)
    def _(i):
        body(pl.ds(pl.multiple_of(i * step, step), step))


class Gather:
    def __init__(self, links, buf, y, c, right, left, sib):
        half = buf.shape[1] // 2
        h0, h1 = pl.ds(0, half), pl.ds(half, half)
        self.links = links
        mine, lb, rb, fb = ((lax.rem(y + d, NY) * 2 + c) for d in (0, 3, 1, 2))

        def cp(block, rows, peer):
            ref = buf.at[block, rows]
            return links.copy(ref, ref, peer)

        self.r0, self.r1 = cp(mine, h0, right), cp(mine, h1, right)
        self.l0, self.l1 = cp(mine, h0, left), cp(mine, h1, left)
        self.fr, self.fl = cp(lb, h0, right), cp(rb, h1, left)
        self.s_own = links.copy(buf.at[mine], buf.at[mine], sib)
        self.s_l0, self.s_l1 = cp(lb, h0, sib), cp(lb, h1, sib)
        self.s_r0, self.s_r1 = cp(rb, h0, sib), cp(rb, h1, sib)
        self.s_f0, self.s_f1 = cp(fb, h0, sib), cp(fb, h1, sib)

    def own(self):
        self.links.start(self.r0, self.l1, self.r1, self.l0, self.s_own)

    def forward(self):
        self.r0.wait_recv()
        self.links.start(self.fr, self.s_l0)
        self.l1.wait_recv()
        self.links.start(self.fl, self.s_r1)

    def middle(self):
        self.r1.wait_recv()
        self.links.start(self.s_l1)
        self.l0.wait_recv()
        self.links.start(self.s_r0)

    def far(self):
        self.fr.wait_recv()
        self.links.start(self.s_f0)
        self.fl.wait_recv()
        self.links.start(self.s_f1)

    def done(self):
        for one in (self.s_own, self.s_l0, self.s_l1, self.s_r0, self.s_r1, self.s_f0, self.s_f1):
            one.wait_recv()


class Ring:
    def __init__(self, links, buf, from_left, from_right, me, right, left, tile):
        n, rows, _ = buf.shape
        self.links, self.buf, self.me, self.n, self.rows, self.tile = links, buf, me, n, rows, tile
        self.fl, self.fr, self.right, self.left = from_left, from_right, right, left
        self.h = h = n // 2
        half = rows // 2
        self.half = half
        a, b = pl.ds(0, half), pl.ds(half, half)
        far = lax.rem(me + h, n)
        rb, lb = lax.rem(me + h - 1, n), lax.rem(me + n - h + 1, n)
        self.rblk, self.lblk = rb, lb
        self.r1 = links.copy(buf.at[far, a], from_left.at[0, a], right)
        self.l1 = links.copy(buf.at[far, b], from_right.at[0, b], left)
        self.r2i = links.copy(buf.at[rb, b], from_left.at[1, b], right)
        self.l2i = links.copy(buf.at[lb, a], from_right.at[1, a], left)
        self.r2d = links.copy(buf.at[rb, a], from_left.at[1, a], right)
        self.l2d = links.copy(buf.at[lb, b], from_right.at[1, b], left)
        self.rs, self.ls = {}, {}
        for s in range(3, h + 1):
            rr, ll = lax.rem(me + h - s + 1, n), lax.rem(me + n - h + s - 1, n)
            self.rs[s] = links.copy(buf.at[rr], from_left.at[s - 1], right)
            self.ls[s] = links.copy(buf.at[ll], from_right.at[s - 1], left)

    def start_far(self):
        self.links.start(self.r1, self.l1)

    def start_near(self):
        self.links.start(self.r2i, self.l2i)

    def start(self):
        self.start_far()
        self.start_near()

    def add(self, block, arrived, first, count):
        tile = min(self.tile, count)

        @pl.loop(0, count // tile)
        def _(i):
            rows = pl.ds(pl.multiple_of(first + i * tile, tile), tile)
            total = self.buf[block, rows].astype(F32) + arrived[rows].astype(F32)
            self.buf[block, rows] = total.astype(BF)

    def arrive(self, s):
        if s == 2:
            for one in (self.r2i, self.r2d, self.l2i, self.l2d):
                one.wait_recv()
        else:
            self.rs[s].wait_recv()
            self.ls[s].wait_recv()

    def step(self, s):
        n, me, h = self.n, self.me, self.h
        if s == 1:
            self.r1.wait_recv()
            self.add(self.rblk, self.fl.at[0], 0, self.half)
            self.links.start(self.r2d)
            self.l1.wait_recv()
            self.add(self.lblk, self.fr.at[0], self.half, self.half)
            self.links.start(self.l2d)
        else:
            if s == 2:
                self.r2i.wait_recv()
                self.r2d.wait_recv()
            else:
                self.rs[s].wait_recv()
            self.add(lax.rem(me + h - s, n), self.fl.at[s - 1], 0, self.rows)
            self.links.start(self.rs[s + 1])
            if s == 2:
                self.l2i.wait_recv()
                self.l2d.wait_recv()
            else:
                self.ls[s].wait_recv()
            self.add(lax.rem(me + n - h + s, n), self.fr.at[s - 1], 0, self.rows)
            self.links.start(self.ls[s + 1])

    def total(self, rows):
        h = self.h
        return (
            self.buf[self.me, rows].astype(F32)
            + self.fl[h - 1, rows].astype(F32)
            + self.fr[h - 1, rows].astype(F32)
        )


class PairRing:
    def __init__(self, links, out, arrived, buf, from_left, from_right, y, right, left, sib, tile):
        self.links, self.arrived, self.y, self.buf, self.tile = links, arrived, y, buf, tile
        self.order = [lax.rem(y + d, NY) for d in (2, 1, 3, 0)]
        self.copies = [links.copy(out.at[i], arrived.at[i], sib) for i in self.order]
        self.ring = Ring(links, buf, from_left, from_right, y, right, left, tile)

    def send(self):
        self.links.start(*self.copies)

    def pair(self, at):
        self.copies[at].wait_recv()
        block = self.order[at]
        self.ring.add(block, self.arrived.at[block], 0, self.ring.rows)

    def start(self):
        self.pair(0)
        self.ring.start_far()
        self.pair(1)
        self.pair(2)
        self.ring.start_near()
        self.pair(3)


def kernel(*refs):
    (dec, cot, mem, lanes, subs, rowinfo, mode, gain, wq_h, wk_h, wv_h, wo_h) = refs[:12]
    (o_layer, o_dec, o_mem, o_q, o_k, o_v, o_o, o_gm) = refs[12:20]
    S = dict(zip(SCRATCH, refs[20 : 20 + len(SCRATCH)]))
    send_sem, recv_sem, local_sem, credit = refs[20 + len(SCRATCH) :]
    links = Links(send_sem, recv_sem)

    dp, tp = lax.axis_index("dp"), lax.axis_index("tensor")
    x, z = dp // NZ, lax.rem(dp, NZ)
    y, c = tp // 2, lax.rem(tp, 2)
    other = 1 - c
    y_right = (dp, lax.rem(y + 1, NY) * 2 + c)
    y_left = (dp, lax.rem(y + 3, NY) * 2 + c)
    sib = (dp, y * 2 + other)
    x_right = (lax.rem(x + 1, NX) * NZ + z, tp)
    x_left = (lax.rem(x + 3, NX) * NZ + z, tp)
    z_right = (x * NZ + lax.rem(z + 1, NZ), tp)
    z_left = (x * NZ + lax.rem(z + 7, NZ), tp)

    weights = [
        pltpu.make_async_copy(src, S[name], local_sem.at[i])
        for i, (src, name) in enumerate(((wq_h, "wq"), (wk_h, "wk"), (wv_h, "wv"), (wo_h, "wo")))
    ]
    for one in weights:
        one.start()

    barrier = pltpu.get_barrier_semaphore()

    @pl.loop(1, NT)
    def _(i):
        pl.semaphore_signal(barrier, 1, device_id=(dp, lax.rem(tp + i, NT)), device_id_type=MESH)

    @pl.loop(1, NDP)
    def _(i):
        pl.semaphore_signal(barrier, 1, device_id=(lax.rem(dp + i, NDP), tp), device_id_type=MESH)

    nall, call, mall = S["nall"], S["call"], S["mall"]
    gather_n = Gather(links, nall, y, c, y_right, y_left, sib)
    gather_m = Gather(links, mall, y, c, y_right, y_left, sib)
    gather_c = Gather(links, call, y, c, y_right, y_left, sib)
    ring_a = PairRing(links, S["sib_out"], S["sib_in"], S["att"], S["att_r"], S["att_l"], y, y_right, y_left, sib, 16)
    ring_g = PairRing(links, S["sib_out"], S["sib_in"], S["gn"], S["gn_r"], S["gn_l"], y, y_right, y_left, sib, 16)
    ring_m = PairRing(links, S["msib_out"], S["msib_in"], S["mt"], S["mt_r"], S["mt_l"], y, y_right, y_left, sib, 64)

    def weight_rings(name, z_first):
        first = (z, z_right, z_left) if z_first else (x, x_right, x_left)
        second = (x, x_right, x_left) if z_first else (z, z_right, z_left)
        one = Ring(links, S[name], S[name + "_r"], S[name + "_l"], *first, 256)
        two = Ring(links, S[name + "2"], S[name + "2_r"], S[name + "2_l"], *second, 128)
        return one, two

    rings = {name: weight_rings(name, name in ("tv", "tq")) for name in ("tv", "to", "tq", "tk")}

    def prepare(rows):
        kind = rowinfo[rows, 1:2]
        m0, m1, m2 = (mode[i : i + 1, :].astype(F32) for i in range(3))
        shifted = dec[rows, :].astype(F32) + jnp.where(kind == 0, m0, jnp.where(kind == 1, m1, m2))
        S["shifted"][rows, :] = shifted
        inv = lax.rsqrt(jnp.mean(shifted * shifted, axis=1, keepdims=True) + 1e-06)
        S["inv"][rows, :] = jnp.broadcast_to(inv, (16, 128))
        nall[tp, rows] = (shifted * inv * gain[...].astype(F32)).astype(BF)
        at = lax.rem(lax.broadcasted_iota(jnp.int32, (16, 1), 0), 16)
        live = at < rowinfo[rows, 0:1]
        call[tp, rows] = jnp.where(live, cot[rows, :].astype(F32), 0.0).astype(BF)

    rows_loop(64, 16, prepare)

    row = lax.broadcasted_iota(jnp.int32, (512, 128), 0)
    lane = lax.broadcasted_iota(jnp.int32, (512, 128), 1)
    row_t = lax.broadcasted_iota(jnp.int32, (128, 512), 0)
    lane_t = lax.broadcasted_iota(jnp.int32, (128, 512), 1)

    def to_owner(which, f):
        hit = (lanes[which : which + 1, :] == row // 16) & (row % 16 == (lane % 4) * 4 + f)
        return jnp.where(hit, 1.0, 0.0).astype(BF)

    def from_owner(which, f):
        hit = (subs[:, which : which + 1] == lane_t // 16) & (lane_t % 16 == (row_t % 4) * 4 + f)
        return jnp.where(hit, 1.0, 0.0).astype(BF)

    def pack(which, source):
        total = None
        for f in range(4):
            term = jnp.dot(to_owner(which, f), source(f), preferred_element_type=F32)
            total = term if total is None else total + term
        return total.astype(BF).reshape(32, 16, 128)

    S["a_out"][...] = pack(0, lambda f: mem[:, f * 128 : f * 128 + 128])
    S["a_in"][dp] = S["a_out"][dp]

    pl.semaphore_wait(barrier, NT - 1 + NDP - 1)

    def exchange(src, dst, count, me, peer, each):
        first = links.take(count)

        @pl.loop(1, count)
        def _(i):
            to = lax.rem(me + i, count)
            pltpu.make_async_remote_copy(
                src_ref=src.at[each(to)],
                dst_ref=dst.at[me],
                send_sem=send_sem.at[first + to],
                recv_sem=recv_sem.at[first + me],
                device_id=peer(to),
                device_id_type=MESH,
            ).start()

        def wait():
            @pl.loop(1, count)
            def _(i):
                come = lax.rem(me + i, count)
                one = pltpu.make_async_remote_copy(
                    src_ref=src.at[each(come)],
                    dst_ref=dst.at[come],
                    send_sem=send_sem.at[first + come],
                    recv_sem=recv_sem.at[first + come],
                    device_id=peer(come),
                    device_id_type=MESH,
                )
                one.wait_send()
                one.wait_recv()

        return wait

    gather_n.own()
    wait_a = exchange(S["a_out"], S["a_in"], NDP, dp, lambda i: (i, tp), lambda i: i)
    wait_a()
    arrived = S["a_in"][...].reshape(512, 128)
    for f in range(4):
        mall[tp, :, f * 128 : f * 128 + 128] = jnp.dot(
            from_owner(0, f), arrived, preferred_element_type=F32
        ).astype(BF)
    gather_m.own()
    gather_n.forward()
    gather_c.own()
    gather_n.middle()
    gather_m.forward()
    gather_m.middle()
    gather_n.far()
    gather_m.far()
    gather_n.done()

    weights[0].wait()

    @pl.loop(0, 2)
    def _(i):
        rows = nall[pl.ds(i * 4, 4)].reshape(256, D)
        S["q"][pl.ds(pl.multiple_of(i * 256, 256), 256), :] = jnp.dot(
            rows, S["wq"][...], preferred_element_type=F32
        ).astype(BF)

    gather_m.done()
    weights[1].wait()
    weights[2].wait()
    for name, weight in (("k", "wk"), ("v", "wv")):
        total = jnp.zeros((128, HD), F32)
        for t in range(8):
            total += jnp.dot(mall[t], S[weight][t * 512 : t * 512 + 512, :], preferred_element_type=F32)
        S[name][...] = total.astype(BF)

    gather_c.forward()

    scores = lax.dot_general(S["q"][...], S["k"][...], NT_DIMS, preferred_element_type=F32) * (HD**-0.5)
    valid = (row // 16 == lane // 4) & (lane % 4 < lanes[2:3, :])
    scores = jnp.where(valid, scores, -1e30)
    expo = jnp.exp(scores - jnp.max(scores, axis=1, keepdims=True))
    expo = jnp.where(valid, expo, 0.0)
    S["p"][...] = expo / jnp.sum(expo, axis=1, keepdims=True)
    context = jnp.dot(S["p"][...].astype(BF), S["v"][...], preferred_element_type=F32)
    S["ctx"][...] = context.astype(BF).reshape(8, 64, HD)
    S["ctx_t"][...] = context.T.astype(BF)

    gather_c.middle()

    def stacked(name, core):
        return jnp.concatenate([S[name][i * 2 + core] for i in range(NY)], axis=0)

    def wide_terms(name, core, dst, product):
        @pl.loop(0, 8)
        def _(i):
            cols = pl.ds(pl.multiple_of(i * 512, 512), 512)
            dst[:, :, cols] = product(stacked(name, core), cols).astype(BF).reshape(NY, 64, 512)

    def by_output(left, cols):
        return jnp.dot(left, S["wo"][:, cols], preferred_element_type=F32)

    def by_query(left, cols):
        return lax.dot_general(left, S["wq"][cols, :], NT_DIMS, preferred_element_type=F32)

    weights[3].wait()
    wide_terms("ctx", other, S["sib_out"], by_output)
    ring_a.send()
    wide_terms("ctx", c, S["att"], by_output)
    gather_c.far()
    ring_a.start()
    pl.semaphore_signal(credit, 1, device_id=sib, device_id_type=MESH)
    gather_c.done()

    @pl.loop(0, 2)
    def _(i):
        rows = call[pl.ds(i * 4, 4)].reshape(256, D)
        S["gctx"][pl.ds(pl.multiple_of(i * 256, 256), 256), :] = lax.dot_general(
            rows, S["wo"][...], NT_DIMS, preferred_element_type=F32
        ).astype(BF)

    probs = S["p"][...]
    grad_v = jnp.dot(probs.T.astype(BF), S["gctx"][...], preferred_element_type=F32)
    S["gv"][...] = grad_v.astype(BF)
    S["gv_t"][...] = grad_v.T.astype(BF)

    def weight_term(name, left, right):
        z_first = name in ("tv", "tq")

        @pl.loop(0, 8)
        def _(i):
            term = jnp.dot(S[left][...], right(i), preferred_element_type=F32).astype(BF)
            tx, tz = i // 2, lax.rem(i, 2) * 4
            for j in range(4):
                block = term[:, j * 128 : j * 128 + 128]
                if z_first:
                    S[name][tz + j, pl.ds(pl.multiple_of(tx * 256, 256), 256)] = block
                else:
                    S[name][tx, pl.ds(pl.multiple_of((tz + j) * 256, 256), 256)] = block

    def wide(ref):
        return lambda i: ref[:, :, pl.ds(pl.multiple_of(i * 512, 512), 512)].reshape(512, 512)

    weight_term("tv", "gv_t", lambda i: mall[i])
    rings["tv"][0].start()
    weight_term("to", "ctx_t", wide(call))
    rings["to"][0].start()

    probs = S["p"][...]
    grad_p = lax.dot_general(S["gctx"][...], S["v"][...], NT_DIMS, preferred_element_type=F32)
    grad_s = probs * (grad_p - jnp.sum(probs * grad_p, axis=1, keepdims=True)) * (HD**-0.5)
    grad_q = jnp.dot(grad_s.astype(BF), S["k"][...], preferred_element_type=F32)
    S["gq"][...] = grad_q.astype(BF).reshape(8, 64, HD)
    S["gq_t"][...] = grad_q.T.astype(BF)
    grad_k = jnp.dot(grad_s.T.astype(BF), S["q"][...], preferred_element_type=F32)
    S["gk"][...] = grad_k.astype(BF)
    S["gk_t"][...] = grad_k.T.astype(BF)

    weight_term("tq", "gq_t", wide(nall))
    rings["tq"][0].start()
    weight_term("tk", "gk_t", lambda i: mall[i])
    rings["tk"][0].start()

    ring_a.ring.step(1)

    for one in ring_a.copies:
        one.wait_send()
    links.started = [one for one in links.started if all(one is not done for done in ring_a.copies)]
    wide_terms("gq", other, S["sib_out"], by_query)
    pl.semaphore_wait(credit, 1)
    ring_g.send()
    wide_terms("gq", c, S["gn"], by_query)
    rings["tv"][0].step(1)
    ring_g.start()

    def memory_terms(core, dst):
        @pl.loop(0, NY)
        def _(i):
            cols = pl.ds(pl.multiple_of((i * 2 + core) * 512, 512), 512)
            term = lax.dot_general(S["gk"][...], S["wk"][cols, :], NT_DIMS, preferred_element_type=F32)
            term += lax.dot_general(S["gv"][...], S["wv"][cols, :], NT_DIMS, preferred_element_type=F32)
            dst[i] = term.astype(BF)

    memory_terms(other, S["msib_out"])
    ring_m.send()
    memory_terms(c, S["mt"])
    rings["to"][0].step(1)
    rings["tq"][0].step(1)
    rings["tk"][0].step(1)
    ring_m.start()

    rings["tv"][0].step(2)

    ring_a.ring.arrive(2)

    def write_layer(rows):
        o_layer[rows, :] = (S["shifted"][rows, :] + ring_a.ring.total(rows)).astype(BF)

    rows_loop(64, 16, write_layer)

    def second(name):
        one, two = rings[name]
        one.arrive(one.h)
        for i in range(two.n):
            two.buf[i] = one.total(pl.ds(i * 256, 256)).astype(BF)
        two.start()

    ring_g.ring.step(1)
    second("to")
    rings["tq"][0].step(2)
    ring_m.ring.step(1)
    rings["tv"][0].step(3)
    second("tk")
    rings["tq"][0].step(3)
    rings["to"][1].step(1)
    rings["tk"][1].step(1)

    S["part"][...] = jnp.zeros_like(S["part"])
    ring_g.ring.arrive(2)

    def write_dec(rows):
        grad = ring_g.ring.total(rows)
        inv = S["inv"][rows, 0:1]
        normed = S["shifted"][rows, :] * inv
        product = grad * normed
        wide_gain = gain[...].astype(F32)
        dot_mean = jnp.mean(wide_gain * product, axis=1, keepdims=True)
        shift = call[tp, rows].astype(F32) + inv * (wide_gain * grad - normed * dot_mean)
        o_dec[rows, :] = shift.astype(BF)
        kind = rowinfo[rows, 1:2]
        S["part"][0] += product[0:8] + product[8:16]
        for i in range(3):
            own = jnp.where(kind == i, shift, 0.0)
            S["part"][i + 1] += own[0:8] + own[8:16]

    rows_loop(64, 16, write_dec)
    for i in range(4):
        total = jnp.sum(S["part"][i], axis=0, keepdims=True)
        for t in range(8):
            S["s_out"][t, i : i + 1, :] = total[:, t * 512 : t * 512 + 256]
            S["s_out"][t, i + 4 : i + 5, :] = total[:, t * 512 + 256 : t * 512 + 512]
    S["s_in"][tp] = S["s_out"][tp]
    wait_s = exchange(S["s_out"], S["s_in"], NT, tp, lambda i: (dp, i), lambda i: i)

    ring_m.ring.arrive(2)
    back = ring_m.ring.total(pl.ds(0, 128)).astype(BF)
    S["b_out"][...] = pack(1, lambda f: back[:, f * 128 : f * 128 + 128])
    S["b_in"][dp] = S["b_out"][dp]
    wait_b = exchange(S["b_out"], S["b_in"], NDP, dp, lambda i: (i, tp), lambda i: i)

    second("tv")
    wait_s()
    S["s_x"][x] = jnp.sum(S["s_in"][...], axis=0)
    wait_x = exchange(S["s_x"], S["s_x"], NX, x, lambda i: (i * NZ + z, tp), lambda i: x)
    second("tq")
    rings["to"][1].step(2)
    rings["tk"][1].step(2)
    wait_x()
    S["s_z"][z] = jnp.sum(S["s_x"][...], axis=0)
    wait_z = exchange(S["s_z"], S["s_z"], NZ, z, lambda i: (x * NZ + i, tp), lambda i: z)
    rings["tv"][1].step(1)
    rings["tq"][1].step(1)
    rings["to"][1].step(3)
    rings["tk"][1].step(3)
    wait_z()
    S["s_all"][tp] = jnp.sum(S["s_z"][...], axis=0)
    wait_t = exchange(S["s_all"], S["s_all"], NT, tp, lambda i: (dp, i), lambda i: tp)

    wait_b()
    arrived = S["b_in"][...].reshape(512, 128)
    for f in range(4):
        o_mem[:, f * 128 : f * 128 + 128] = jnp.dot(
            from_owner(1, f), arrived, preferred_element_type=F32
        ).astype(BF)

    for name, dst in (("tv", o_v), ("tq", o_q), ("to", o_o), ("tk", o_k)):
        ring = rings[name][1]
        ring.arrive(ring.h)
        total = ring.total(pl.ds(0, 256))
        dst[...] = (total if name == "to" else total.T).astype(BF)

    wait_t()
    for t in range(8):
        o_gm[:, t * 512 : t * 512 + 256] = S["s_all"][t, 0:4, :]
        o_gm[:, t * 512 + 256 : t * 512 + 512] = S["s_all"][t, 4:8, :]
    links.finish_sends()


def shards(
    decoder_states,
    encoder_memory,
    memory_route,
    memory_length,
    target_length,
    objective,
    mode_table,
    norm_gain,
    w_query,
    w_key,
    w_value,
    w_output,
    cotangent,
):
    me = lax.axis_index("dp")
    own_owner = lax.dynamic_slice_in_dim(memory_route, me * 32, 32, 0) // 32
    hit = memory_route[None, :] == (me * 32 + jnp.arange(32, dtype=jnp.int32))[:, None]
    source = jnp.sum(jnp.where(hit, jnp.arange(1024, dtype=jnp.int32)[None, :] // 32, 0), axis=1)
    length = jnp.sum(jnp.where(hit, memory_length[None, :], 0), axis=1)
    lanes = jnp.repeat(jnp.stack([own_owner, source, length]), 4, axis=1)
    subs = jnp.repeat(jnp.stack([source, own_owner], axis=1), 4, axis=0)
    rowinfo = jnp.repeat(jnp.stack([target_length, objective], axis=1), 16, axis=0)

    vmem = pl.BlockSpec(memory_space=pltpu.VMEM)
    hbm = pl.BlockSpec(memory_space=pl.ANY)
    shape = jax.ShapeDtypeStruct
    layer, dec, mem, gq, gk, gv, go, gm = pl.pallas_call(
        kernel,
        out_shape=[
            shape((64, D), BF),
            shape((64, D), BF),
            shape((128, 512), BF),
            shape((128, HD), BF),
            shape((128, HD), BF),
            shape((128, HD), BF),
            shape((HD, 128), BF),
            shape((4, D), F32),
        ],
        in_specs=[vmem] * 8 + [hbm] * 4,
        out_specs=[vmem] * 8,
        scratch_shapes=[pltpu.VMEM(*spec) for spec in SCRATCH.values()]
        + [
            pltpu.SemaphoreType.DMA((NSEM,)),
            pltpu.SemaphoreType.DMA((NSEM,)),
            pltpu.SemaphoreType.DMA((4,)),
            pltpu.SemaphoreType.REGULAR,
        ],
        compiler_params=pltpu.CompilerParams(
            collective_id=0, has_side_effects=True, vmem_limit_bytes=62 * 1024 * 1024
        ),
        cost_estimate=pl.CostEstimate(flops=8 * 10**9, bytes_accessed=12 * 10**6, transcendentals=10**5),
    )(
        decoder_states.reshape(64, D),
        cotangent.reshape(64, D),
        encoder_memory.reshape(128, 512),
        lanes,
        subs,
        rowinfo,
        mode_table,
        norm_gain.reshape(1, D),
        w_query,
        w_key,
        w_value,
        w_output,
    )
    return (
        layer.reshape(4, 16, D),
        dec.reshape(4, 16, D),
        mem.reshape(32, 4, 512),
        gq,
        gk,
        gv,
        go,
        gm[0],
        gm[1:4],
    )


def solution(mesh):
    return jax.shard_map(
        shards,
        mesh=mesh,
        in_specs=(
            P(("dp", "tensor"), None, None),
            P("dp", None, "tensor"),
            P(),
            P(),
            P(("dp", "tensor")),
            P(("dp", "tensor")),
            P(),
            P(),
            P(None, "tensor"),
            P(None, "tensor"),
            P(None, "tensor"),
            P("tensor", None),
            P(("dp", "tensor"), None, None),
        ),
        out_specs=(
            P(("dp", "tensor"), None, None),
            P(("dp", "tensor"), None, None),
            P("dp", None, "tensor"),
            P("dp", "tensor"),
            P("dp", "tensor"),
            P("dp", "tensor"),
            P("tensor", "dp"),
            P(),
            P(),
        ),
        check_vma=False,
    )
```

time: 1400 us -> 158 us (0.11)
  waiting for transfers between devices: 1270 us -> 0 us
  Pallas kernels: 0 us -> 138 us
  matrix products: 45.6 us -> 0 us
  starting transfers between devices: 22.1 us -> 0 us
  other arithmetic: 19.6 us -> 3.15 us
    reduce_scatter x6 -> x0, waiting for transfers between devices: 722 us -> none  [the longest x1 219 us: shards(): lax.psum_scatter(weight_terms[2].astype(jnp.bfloat16), 'dp', scatter_dime...]
    psum x1 -> x0, waiting for transfers between devices: 251 us -> none  [shards(): grad_gain, grad_mode = lax.psum((gain_term, mode_term), ('dp', 'tensor'))]
    unnamed x12 -> x0, waiting for transfers between devices: 211 us -> none
    pallas_call x0 -> x1, Pallas kernels: none -> 138 us  [shards(): pl.pallas_call(kernel, out_shape=[shape((64, D), BF), shape((64, D), BF),...]
    all_gather x3 -> x0, waiting for transfers between devices: 85.7 us -> none  [the longest x1 33.7 us: shards(): all_normed = lax.all_gather(normed_in, 'tensor', axis=0, tiled=True)]
    dot_general x20 -> x0, matrix products: 45.6 us -> none  [the longest x1 4.85 us: shards(): jnp.einsum('btd,wd->btw', all_cot, w_output, preferred_element_type=jnp.f...]
    all_to_all x2 -> x0, starting transfers between devices: 21.4 us -> none  [the longest x1 11.9 us: shards(): lax.all_to_all(send_rows, 'dp', split_axis=0, concat_axis=0, tiled=True)]
  transfers between devices with their start and end apart: 13 -> 0, of which waited for: 11 -> 0; matrix products, arithmetic and copies ran while one was open for 4% -> 0% of each run, Pallas kernels for 0% -> 0%
where the time goes in v1:
time: 158 us
  Pallas kernels  138 us (87%)
  local copies, waits for them, and re-layouts  16 us (10%)
  other arithmetic  3.15 us (2%)
    pallas_call x1, Pallas kernels, shards(): pl.pallas_call(kernel, out_shape=[shape((64, D), BF), shape((64, D), BF),...  138 us
    unnamed x15, local copies, waits for them, and re-layouts  6.36 us

profile of v1, /device:TPU:1, one launch (start us, length us, event | category | flops | bytes accessed | tf_op | source)
XLA Modules:
  0.0 157.8 jit_solution(1652928974722853381)
XLA Ops:
  0.7 0.8 fusion.5
  1.4 0.8 fusion.6
  2.2 0.7 pad_add_fusion.2
  2.9 0.1 copy.29
  3.0 0.9 fusion
  3.9 0.1 copy.26
  4.0 1.3 reshape.97.refs_7_
  5.3 0.6 broadcast_in_dim.36.clone
  5.9 0.1 broadcast_in_dim.34
  6.0 0.7 reshape.94.refs_3_
  6.7 0.6 broadcast_in_dim.35
  7.3 1.6 %reshape.93.refs_2_ = bf16[128,512]{1,0:T(8,128)(2,1)} reshape(bf16[32,4,512]{2,1,0:T(4,128)(2,1)} %param.14) | data formatting | bytes 262144 | tf_op jit(solution)/shard_map/reshape | solution.py:702
  8.9 138.0 %shard_map.196 = (bf16[64,4096]{1,0:T(8,128)(2,1)}, bf16[64,4096]{1,0:T(8,128)(2,1)}, bf16[128,512]{1,0:T(8,128)(2,1)}, bf16[128,256]{1,0:T(8,128)(2,1)}, bf16[1...) custom-call(bf16[64,4096]{1,0:T(8,128)(2,1)} %bitcast.26, ...), custom_call_target="tpu_custom_call" | custom-call | flops 8000000000 | bytes 12000000 | tf_op jit(solution)/shard_map/pallas_call | solution.py:674
  146.9 0.0 copy-start.3
  147.0 0.0 copy-start.2
  147.0 0.0 copy-start.1
  147.0 0.0 copy-start
  147.0 1.5 slice.6
  148.5 1.5 slice.7
  150.0 1.6 %reshape.100 = bf16[32,4,512]{2,1,0:T(4,128)(2,1)} reshape(bf16[128,512]{1,0:T(8,128)(2,1)} %get-tuple-element.19) | data formatting | bytes 262144 | tf_op jit(solution)/shard_map/reshape | solution.py:716
  151.6 1.9 %copy.36 = bf16[4,16,4096]{2,1,0:T(8,128)(2,1)} copy(bf16[4,16,4096]{2,1,0:T(8,128)(2,1)} %bitcast.17) | data formatting | bytes 1048576
  153.4 1.9 %copy.37 = bf16[4,16,4096]{2,1,0:T(8,128)(2,1)} copy(bf16[4,16,4096]{2,1,0:T(8,128)(2,1)} %bitcast.16) | data formatting | bytes 1048576
  155.3 0.0 copy-done.3
  155.3 0.6 copy.38
  155.9 0.0 copy-done.2
  155.9 0.6 copy.39
  156.6 0.0 copy-done.1
  156.6 0.6 copy.40
  157.2 0.0 copy-done
  157.2 0.6 copy.41
  (4 shorter events, 0.0 us)
Async XLA Ops:
  146.9 8.4 %copy-start.3 = (bf16[128,256]{1,0:T(8,128)(2,1)S(1)}, bf16[128,256]{1,0:T(8,128)(2,1)}, u32[]{:S(2)}) copy-start(bf16[128,256]{1,0:T(8,128)(2,1)} %get-tuple-element.39) | copy-start | bytes 196612
  147.0 9.0 %copy-start.2 = (bf16[128,256]{1,0:T(8,128)(2,1)S(1)}, bf16[128,256]{1,0:T(8,128)(2,1)}, u32[]{:S(2)}) copy-start(bf16[128,256]{1,0:T(8,128)(2,1)} %get-tuple-element.40) | copy-start | bytes 196612
  147.0 9.6 %copy-start.1 = (bf16[128,256]{1,0:T(8,128)(2,1)S(1)}, bf16[128,256]{1,0:T(8,128)(2,1)}, u32[]{:S(2)}) copy-start(bf16[128,256]{1,0:T(8,128)(2,1)} %get-tuple-element.41) | copy-start | bytes 196612
  147.0 10.2 %copy-start = (bf16[256,128]{1,0:T(8,128)(2,1)S(1)}, bf16[256,128]{1,0:T(8,128)(2,1)}, u32[]{:S(2)}) copy-start(bf16[256,128]{1,0:T(8,128)(2,1)} %get-tuple-element.42) | copy-start | bytes 196612

commit v2 on v0

v2 whole, which is shorter than its diff:
```python
import types

import jax
import jax.numpy as jnp
from jax import lax
from jax.experimental import pallas as pl
from jax.experimental.pallas import tpu as pltpu
from jax.sharding import PartitionSpec as P

HD = 256
D = 4096
NX, NZ, NY = 4, 8, 4
NDP, NT = 32, 8
BF = jnp.bfloat16
F32 = jnp.float32
MESH = pl.DeviceIdType.MESH
NT_DIMS = (((1,), (1,)), ((), ()))

SOURCES = dict(
    i_mode=((3, D), BF),
    i_gain=((32, 128), BF),
    i_dec=((4, 16, D), BF),
    i_route=((8, 128), jnp.int32),
    i_lengths=((8, 128), jnp.int32),
    i_mem=((32, 4, 512), BF),
    i_cot=((4, 16, D), BF),
    wq=((D, HD), BF),
    wk=((D, HD), BF),
    wv=((D, HD), BF),
    wo=((HD, D), BF),
)
RESULTS = dict(
    r_layer=((4, 16, D), BF),
    r_dec=((4, 16, D), BF),
    r_mem=((32, 4, 512), BF),
    r_q=((128, HD), BF),
    r_k=((128, HD), BF),
    r_v=((128, HD), BF),
    r_o=((HD, 128), BF),
    r_gain=((32, 128), F32),
    r_mode=((3, D), F32),
)
BUFFERS = dict(
    nall=((8, 64, D), BF),
    call=((2, 8, 64, D // 2), BF),
    mall=((8, 128, 512), BF),
    a_out=((32, 16, 128), BF),
    a_in=((32, 16, 128), BF),
    b_out=((32, 16, 128), BF),
    b_in=((32, 16, 128), BF),
    shifted=((64, D), F32),
    inv=((64, 128), F32),
    q=((512, HD), BF),
    k=((128, HD), BF),
    v=((128, HD), BF),
    ctx=((8, 64, HD), BF),
    gctx=((512, HD), BF),
    gq=((8, 64, HD), BF),
    gk=((128, HD), BF),
    gv=((128, HD), BF),
    ctx_t=((HD, 512), BF),
    gq_t=((HD, 512), BF),
    gk_t=((HD, 128), BF),
    gv_t=((HD, 128), BF),
    p=((512, 128), F32),
    sib_out=((4, 64, D), BF),
    sib_in=((4, 64, D), BF),
    att=((4, 64, D), BF),
    att_r=((2, 64, D), BF),
    att_l=((2, 64, D), BF),
    gn=((4, 64, D), BF),
    gn_r=((2, 64, D), BF),
    gn_l=((2, 64, D), BF),
    msib_out=((4, 128, 512), BF),
    msib_in=((4, 128, 512), BF),
    mt=((4, 128, 512), BF),
    mt_r=((2, 128, 512), BF),
    mt_l=((2, 128, 512), BF),
    part=((4, 8, D), F32),
    s_out=((8, 8, 256), F32),
    s_in=((8, 8, 256), F32),
    s_x=((4, 8, 256), F32),
    s_z=((8, 8, 256), F32),
    s_all=((8, 8, 256), F32),
    gain=((1, D), F32),
    lanes=((128, 128), F32),
    cols=((128, 128), F32),
    back=((32, 4, 512), F32),
)
SCRATCH = SOURCES | RESULTS | BUFFERS
X_ROWS = (160, 160, 160, 128)

NSEND, NRECV = 32, 85


def ring_buffers(n, rows):
    return [((n, rows, 128), BF), ((n // 2, rows, 128), BF), ((n // 2, rows, 128), BF)]


def term_buffers(xr):
    zr = HD - xr
    found = ring_buffers(NX, NZ * xr) + ring_buffers(NZ, xr)
    return found + (ring_buffers(NZ, NX * zr) + ring_buffers(NX, zr) if zr else [])


TERM_BUFFERS = [term_buffers(xr) for xr in X_ROWS]
FLAT = list(SCRATCH.values()) + [one for term in TERM_BUFFERS for one in term]


class Links:
    def __init__(self, send, recv):
        self.send, self.recv, self.sends, self.recvs, self.open = send, recv, 0, 0, []

    def new_send(self):
        self.sends += 1
        assert self.sends <= NSEND
        return self.sends - 1

    def new_recv(self):
        self.recvs += 1
        assert self.recvs <= NRECV
        return self.recvs - 1

    def copy(self, src, dst, send, recv, peer):
        return pltpu.make_async_remote_copy(
            src_ref=src,
            dst_ref=dst,
            send_sem=self.send.at[send],
            recv_sem=self.recv.at[recv],
            device_id=peer,
            device_id_type=MESH,
        )

    def arrived(self, recv, ref, peer):
        self.copy(ref, ref, 0, recv, peer).wait_recv()

    def sent(self, send, ref, peer):
        self.copy(ref, ref, send, 0, peer).wait_send()

    def finish_sends(self):
        for one in self.open:
            self.sent(*one)
        self.open = []


class Gather:
    def __init__(self, links, buf, y, c, right, left, sib):
        half = buf.shape[1] // 2
        self.h0, self.h1 = pl.ds(0, half), pl.ds(half, half)
        self.links, self.buf, self.complete = links, buf, False
        self.right, self.left, self.sib = right, left, sib
        self.mine, self.lb, self.rb, self.fb = (lax.rem(y + d, NY) * 2 + c for d in (0, 3, 1, 2))
        self.send = links.new_send()
        self.near, self.mid, self.last, self.pair = (links.new_recv() for _ in range(4))

    def push(self, block, rows, recv, peer):
        ref = self.buf.at[block, rows]
        self.links.copy(ref, ref, self.send, recv, peer).start()

    def wait(self, recv, blocks):
        self.links.arrived(recv, self.buf.at[pl.ds(0, blocks)], self.sib)

    def own(self):
        self.push(self.mine, self.h0, self.near, self.right)
        self.push(self.mine, self.h1, self.near, self.left)
        self.push(self.mine, self.h1, self.mid, self.right)
        self.push(self.mine, self.h0, self.mid, self.left)
        ref = self.buf.at[self.mine]
        self.links.copy(ref, ref, self.send, self.pair, self.sib).start()
        self.links.open.append((self.send, self.buf.at[pl.ds(0, 7)], self.sib))

    def forward(self):
        self.wait(self.near, 1)
        self.push(self.lb, self.h0, self.last, self.right)
        self.push(self.rb, self.h1, self.last, self.left)
        self.push(self.lb, self.h0, self.pair, self.sib)
        self.push(self.rb, self.h1, self.pair, self.sib)

    def middle(self):
        self.wait(self.mid, 1)
        self.push(self.lb, self.h1, self.pair, self.sib)
        self.push(self.rb, self.h0, self.pair, self.sib)

    def far(self):
        self.wait(self.last, 1)
        self.push(self.fb, self.h0, self.pair, self.sib)
        self.push(self.fb, self.h1, self.pair, self.sib)

    def done(self):
        if not self.complete:
            self.complete = True
            self.wait(self.pair, 4)


class Ring:
    def __init__(self, links, buf, from_left, from_right, me, right, left, tile):
        self.n, self.rows, _ = buf.shape
        self.links, self.buf, self.me, self.tile = links, buf, me, tile
        self.fl, self.fr, self.right, self.left = from_left, from_right, right, left
        self.h = self.n // 2
        self.half = self.rows // 2
        self.a, self.b = pl.ds(0, self.half), pl.ds(self.half, self.half)
        self.send = links.new_send()
        self.stage = [None] + [links.new_recv() for _ in range(self.h)]

    def at(self, distance):
        return lax.rem(self.me + distance + self.n, self.n)

    def push_right(self, stage, rows):
        src = self.buf.at[self.at(self.h + 1 - stage), rows]
        self.links.copy(src, self.fl.at[stage - 1, rows], self.send, self.stage[stage], self.right).start()

    def push_left(self, stage, rows):
        src = self.buf.at[self.at(stage - 1 - self.h), rows]
        self.links.copy(src, self.fr.at[stage - 1, rows], self.send, self.stage[stage], self.left).start()

    def start_far(self):
        self.push_right(1, self.a)
        self.push_left(1, self.b)
        self.links.open.append((self.send, self.buf.at[pl.ds(0, self.n - 1)], self.right))

    def start_near(self):
        self.push_right(2, self.b)
        self.push_left(2, self.a)

    def start(self):
        self.start_far()
        self.start_near()

    def add(self, block, arrived, first, count):
        tile = min(self.tile, count)

        @pl.loop(0, count // tile)
        def _(i):
            rows = pl.ds(pl.multiple_of(first + i * tile, tile), tile)
            total = self.buf[block, rows].astype(F32) + arrived[rows].astype(F32)
            self.buf[block, rows] = total.astype(BF)

    def arrive(self, stage):
        blocks = 1 if stage == 1 else 2
        self.links.arrived(self.stage[stage], self.buf.at[pl.ds(0, blocks)], self.right)

    def step(self, stage):
        self.arrive(stage)
        whole = pl.ds(0, self.rows)
        if stage == 1:
            self.add(self.at(self.h - 1), self.fl.at[0], 0, self.half)
            self.push_right(2, self.a)
            self.add(self.at(1 - self.h), self.fr.at[0], self.half, self.half)
            self.push_left(2, self.b)
        else:
            self.add(self.at(self.h - stage), self.fl.at[stage - 1], 0, self.rows)
            self.push_right(stage + 1, whole)
            self.add(self.at(stage - self.h), self.fr.at[stage - 1], 0, self.rows)
            self.push_left(stage + 1, whole)

    def total(self, rows):
        h = self.h
        return (
            self.buf[self.me, rows].astype(F32)
            + self.fl[h - 1, rows].astype(F32)
            + self.fr[h - 1, rows].astype(F32)
        )


class PairRing:
    def __init__(self, links, out, arrived, buf, from_left, from_right, y, right, left, sib, tile):
        self.links, self.out, self.arrived, self.sib = links, out, arrived, sib
        self.order = [lax.rem(y + d, NY) for d in (2, 1, 3, 0)]
        self.sending = links.new_send()
        self.coming = [links.new_recv() for _ in range(3)]
        self.ring = Ring(links, buf, from_left, from_right, y, right, left, tile)

    def send(self):
        for i, recv in zip(self.order, (0, 1, 1, 2)):
            self.links.copy(self.out.at[i], self.arrived.at[i], self.sending, self.coming[recv], self.sib).start()
        self.links.open.append((self.sending, self.out, self.sib))

    def sent(self):
        self.links.sent(self.sending, self.out, self.sib)
        self.links.open = [one for one in self.links.open if one[0] != self.sending]

    def pair(self, recv, blocks):
        self.links.arrived(self.coming[recv], self.arrived.at[pl.ds(0, len(blocks))], self.sib)
        for block in blocks:
            self.ring.add(block, self.arrived.at[block], 0, self.ring.rows)

    def start(self):
        self.pair(0, self.order[:1])
        self.ring.start_far()
        self.pair(1, self.order[1:3])
        self.ring.start_near()
        self.pair(2, self.order[3:])


class Term:
    def __init__(self, links, xr, refs, x, z, on_x, on_z, left, right, out, flip):
        self.x, self.xr, self.zr, self.left, self.right, self.out, self.flip = x, xr, HD - xr, left, right, out, flip
        zr = self.zr
        self.xf = Ring(links, *refs[0:3], *on_x, 2 * xr)
        self.xs = Ring(links, *refs[3:6], *on_z, xr // 2)
        self.zf = self.zs = None
        if zr:
            self.zf = Ring(links, *refs[6:9], *on_z, 2 * zr)
            self.zs = Ring(links, *refs[9:12], *on_x, zr // 2)

    def tile(self, tx, half):
        term = jnp.dot(self.left[...], self.right(tx, half), preferred_element_type=F32).astype(BF)
        for j in range(4):
            tz = half * 4 + j
            block = term[:, j * 128 : j * 128 + 128]
            self.xf.buf[tx, pl.ds(pl.multiple_of(tz * self.xr, self.xr), self.xr)] = block[0 : self.xr]
            if self.zr:
                self.zf.buf[tz, pl.ds(pl.multiple_of(tx * self.zr, self.zr), self.zr)] = block[self.xr :]

    def first(self):
        @pl.loop(0, 2)
        def _(i):
            self.tile(lax.rem(self.x + 2, NX), i)

        self.xf.start_far()

    def near(self):
        @pl.loop(0, 4)
        def _(i):
            self.tile(lax.rem(self.x + 1 + (i // 2) * 2, NX), lax.rem(i, 2))

        self.xf.start_near()

    def own(self):
        @pl.loop(0, 2)
        def _(i):
            self.tile(self.x, i)

        if self.zr:
            self.zf.start()

    def second(self, one, two, rows):
        one.arrive(one.h)
        for i in range(two.n):
            two.buf[i] = one.total(pl.ds(i * rows, rows)).astype(BF)
        two.start()

    def to_z(self):
        self.second(self.xf, self.xs, self.xr)

    def to_x(self):
        self.second(self.zf, self.zs, self.zr)

    def result(self, copy):
        parts = [(self.xs, self.xr)] + ([(self.zs, self.zr)] if self.zr else [])
        for ring, _ in parts:
            ring.arrive(ring.h)
        total = jnp.concatenate([ring.total(pl.ds(0, rows)) for ring, rows in parts], axis=0)
        self.out[...] = (total.T if self.flip else total).astype(BF)
        copy.start()


def kernel(*refs):
    target, objective = refs[:2]
    count = len(SOURCES), len(RESULTS), len(SCRATCH), len(FLAT)
    sources, outs = refs[2 : 2 + count[0]], refs[2 + count[0] : 2 + count[0] + count[1]]
    held = refs[2 + count[0] + count[1] :]
    S = types.SimpleNamespace(**dict(zip(SCRATCH, held)))
    of_terms = iter(held[count[2] : count[3]])
    send_sem, recv_sem, local_sem, credit = held[count[3] :]
    links = Links(send_sem, recv_sem)

    dp, tp = lax.axis_index("dp"), lax.axis_index("tensor")
    x, z = dp // NZ, lax.rem(dp, NZ)
    y, c = tp // 2, lax.rem(tp, 2)
    other = 1 - c
    y_right = (dp, lax.rem(y + 1, NY) * 2 + c)
    y_left = (dp, lax.rem(y + 3, NY) * 2 + c)
    sib = (dp, y * 2 + other)
    x_right = (lax.rem(x + 1, NX) * NZ + z, tp)
    x_left = (lax.rem(x + 3, NX) * NZ + z, tp)
    z_right = (x * NZ + lax.rem(z + 1, NZ), tp)
    z_left = (x * NZ + lax.rem(z + 7, NZ), tp)

    arriving, results = types.SimpleNamespace(), types.SimpleNamespace()
    for i, name in enumerate(SOURCES):
        setattr(arriving, name, pltpu.make_async_copy(sources[i], held[i], local_sem.at[i]))
    for i, name in enumerate(RESULTS):
        copy = pltpu.make_async_copy(held[count[0] + i], outs[i], local_sem.at[count[0] + i])
        setattr(results, name, copy)
    loaded = list(vars(arriving).values())
    for one in loaded[:3]:
        one.start()

    def need(*copies):
        for one in copies:
            if any(one is other for other in loaded):
                loaded[:] = [other for other in loaded if other is not one]
                one.wait()

    barrier = pltpu.get_barrier_semaphore()

    @pl.loop(1, NT)
    def _(i):
        pl.semaphore_signal(barrier, 1, device_id=(dp, lax.rem(tp + i, NT)), device_id_type=MESH)

    @pl.loop(1, NDP)
    def _(i):
        pl.semaphore_signal(barrier, 1, device_id=(lax.rem(dp + i, NDP), tp), device_id_type=MESH)

    for one in loaded[3:]:
        one.start()

    nall, call, mall = S.nall, S.call, S.mall
    gather_n = Gather(links, nall, y, c, y_right, y_left, sib)
    gather_m = Gather(links, mall, y, c, y_right, y_left, sib)
    early = 1 - x // 2
    gather_0 = Gather(links, call.at[early], y, c, y_right, y_left, sib)
    gather_1 = Gather(links, call.at[1 - early], y, c, y_right, y_left, sib)
    ring_a = PairRing(links, S.sib_out, S.sib_in, S.att, S.att_r, S.att_l, y, y_right, y_left, sib, 16)
    ring_g = PairRing(links, S.sib_out, S.sib_in, S.gn, S.gn_r, S.gn_l, y, y_right, y_left, sib, 16)
    ring_m = PairRing(links, S.msib_out, S.msib_in, S.mt, S.mt_r, S.mt_l, y, y_right, y_left, sib, 64)

    def by_context(tx, half):
        cols = pl.ds(pl.multiple_of(lax.rem(tx, 2) * 1024 + half * 512, 512), 512)
        return call[tx // 2, :, :, cols].reshape(512, 512)

    def by_normed(tx, half):
        return nall[:, :, pl.ds(pl.multiple_of(tx * 1024 + half * 512, 512), 512)].reshape(512, 512)

    def by_memory(tx, half):
        return mall[tx * 2 + half]

    on_x, on_z = (x, x_right, x_left), (z, z_right, z_left)
    to, tv, tq, tk = (
        Term(links, xr, [next(of_terms) for _ in spec], x, z, on_x, on_z, left, right, out, flip)
        for xr, spec, left, right, out, flip in zip(
            X_ROWS,
            TERM_BUFFERS,
            (S.ctx_t, S.gv_t, S.gq_t, S.gk_t),
            (by_context, by_memory, by_normed, by_memory),
            (S.r_o, S.r_v, S.r_q, S.r_k),
            (False, True, True, True),
        )
    )

    need(arriving.i_mode, arriving.i_gain, arriving.i_dec)
    wide_gain = jnp.concatenate([S.i_gain[i : i + 1, :].astype(F32) for i in range(32)], axis=1)
    S.gain[...] = wide_gain

    @pl.loop(0, 4)
    def _(i):
        rows = pl.ds(pl.multiple_of(i * 16, 16), 16)
        kind = jnp.full((1, D), objective[i], jnp.int32)
        m0, m1, m2 = (S.i_mode[j : j + 1, :].astype(F32) for j in range(3))
        shifted = S.i_dec[i].astype(F32) + jnp.where(kind == 0, m0, jnp.where(kind == 1, m1, m2))
        S.shifted[rows, :] = shifted
        inv = lax.rsqrt(jnp.mean(shifted * shifted, axis=1, keepdims=True) + 1e-06)
        S.inv[rows, :] = jnp.broadcast_to(inv, (16, 128))
        nall[tp, rows] = (shifted * inv * S.gain[...]).astype(BF)

    pl.semaphore_wait(barrier, NT - 1 + NDP - 1)

    row = lax.broadcasted_iota(jnp.int32, (512, 128), 0)
    lane = lax.broadcasted_iota(jnp.int32, (512, 128), 1)
    row_t = lax.broadcasted_iota(jnp.int32, (128, 512), 0)
    lane_t = lax.broadcasted_iota(jnp.int32, (128, 512), 1)

    def pack(which, rows):
        total = None
        match = S.lanes[which : which + 1, :].astype(jnp.int32) == row // 16
        for f in range(4):
            hot = jnp.where(match & (row % 16 == (lane // 32) * 4 + f), 1.0, 0.0).astype(BF)
            term = jnp.dot(hot, rows[:, f * 128 : f * 128 + 128], preferred_element_type=F32)
            total = term if total is None else total + term
        return total.astype(BF).reshape(32, 16, 128)

    def unpack(which, packed):
        match = S.cols[:, which : which + 1].astype(jnp.int32) == lane_t // 16
        parts = []
        for f in range(4):
            hot = jnp.where(match & (lane_t % 16 == (row_t // 32) * 4 + f), 1.0, 0.0).astype(BF)
            parts.append(jnp.dot(hot, packed, preferred_element_type=F32))
        return jnp.concatenate(parts, axis=1)

    def exchange(src, dst, count, me, peer, each):
        send, recv = links.new_send(), links.new_recv()

        @pl.loop(1, count)
        def _(i):
            to = lax.rem(me + i, count)
            links.copy(src.at[each(to)], dst.at[me], send, recv, peer(to)).start()

        def wait():
            others = dst.at[pl.ds(0, count - 1)]
            links.sent(send, others, sib)
            links.arrived(recv, others, sib)

        return wait

    waits = types.SimpleNamespace()

    def send_examples():
        need(arriving.i_route, arriving.i_lengths, arriving.i_mem)
        at = lax.broadcasted_iota(jnp.int32, (32, 128), 1)
        entry = dp * 32 + lax.broadcasted_iota(jnp.int32, (32, 128), 0)
        owner = source = length = jnp.zeros((32, 128), F32)
        for i in range(8):
            slots = S.i_route[i : i + 1, :]
            owner += jnp.where(at + i * 128 == entry, (slots // 32).astype(F32), 0.0)
            source += jnp.where(slots == entry, ((at + i * 128) // 32).astype(F32), 0.0)
            length += jnp.where(slots == entry, S.i_lengths[i : i + 1, :].astype(F32), 0.0)

        def column(table):
            return jnp.concatenate([jnp.sum(table, axis=1, keepdims=True)] * 4, axis=0)

        at = lax.broadcasted_iota(jnp.int32, (128, 128), 1)
        S.cols[...] = jnp.where(at == 0, column(owner), jnp.where(at == 1, column(source), column(length)))
        S.lanes[...] = S.cols[...].T
        own_rows = S.i_mem[...].astype(F32)
        S.a_out[...] = pack(0, jnp.concatenate([own_rows[:, j, :] for j in range(4)], axis=0).astype(BF))
        S.a_in[dp] = S.a_out[dp]
        waits.a = exchange(S.a_out, S.a_in, NDP, dp, lambda i: (i, tp), lambda i: i)

    def mask_cotangent():
        need(arriving.i_cot)

        @pl.loop(0, 4)
        def _(i):
            rows = pl.ds(pl.multiple_of(i * 16, 16), 16)
            live = lax.broadcasted_iota(jnp.int32, (16, D), 0) < jnp.full((16, D), target[i], jnp.int32)
            masked = jnp.where(live, S.i_cot[i].astype(F32), 0.0).astype(BF)
            for j in range(2):
                call[j, tp, rows] = masked[:, j * 2048 : j * 2048 + 2048]

    def place_examples():
        waits.a()
        mall[tp] = unpack(1, S.a_in[...].reshape(512, 128)).astype(BF)

    def queries():
        gather_n.done()
        need(arriving.wq)

        @pl.loop(0, 2)
        def _(i):
            rows = nall[pl.ds(i * 4, 4)].reshape(256, D)
            S.q[pl.ds(pl.multiple_of(i * 256, 256), 256), :] = jnp.dot(
                rows, S.wq[...], preferred_element_type=F32
            ).astype(BF)

    def keys_values():
        gather_m.done()
        need(arriving.wk, arriving.wv)
        for out, weight in ((S.k, S.wk), (S.v, S.wv)):
            total = jnp.zeros((128, HD), F32)
            for t in range(8):
                total += jnp.dot(mall[t], weight[t * 512 : t * 512 + 512, :], preferred_element_type=F32)
            out[...] = total.astype(BF)

    def attention():
        scores = lax.dot_general(S.q[...], S.k[...], NT_DIMS, preferred_element_type=F32) * (HD**-0.5)
        valid = (row // 16 == lane % 32) & (lane // 32 < S.lanes[2:3, :].astype(jnp.int32))
        scores = jnp.where(valid, scores, -1e30)
        expo = jnp.exp(scores - jnp.max(scores, axis=1, keepdims=True))
        expo = jnp.where(valid, expo, 0.0)
        S.p[...] = expo / jnp.sum(expo, axis=1, keepdims=True)
        context = jnp.dot(S.p[...].astype(BF), S.v[...], preferred_element_type=F32)
        S.ctx[...] = context.astype(BF).reshape(8, 64, HD)
        S.ctx_t[...] = context.T.astype(BF)

    def stacked(ref, core):
        return jnp.concatenate([ref[i * 2 + core] for i in range(NY)], axis=0)

    def wide_terms(ref, core, dst, product):
        @pl.loop(0, 8)
        def _(i):
            cols = pl.ds(pl.multiple_of(i * 512, 512), 512)
            dst[:, :, cols] = product(stacked(ref, core), cols).astype(BF).reshape(NY, 64, 512)

    def by_output(left, cols):
        need(arriving.wo)
        return jnp.dot(left, S.wo[:, cols], preferred_element_type=F32)

    def by_query(left, cols):
        return lax.dot_general(left, S.wq[cols, :], NT_DIMS, preferred_element_type=F32)

    def output_other():
        need(arriving.wo)
        wide_terms(S.ctx, other, S.sib_out, by_output)
        ring_a.send()

    def output_own():
        wide_terms(S.ctx, c, S.att, by_output)

    def output_ring():
        ring_a.start()
        pl.semaphore_signal(credit, 1, device_id=sib, device_id_type=MESH)

    def normed_other():
        ring_a.sent()
        wide_terms(S.gq, other, S.sib_out, by_query)
        pl.semaphore_wait(credit, 1)
        ring_g.send()

    def normed_own():
        wide_terms(S.gq, c, S.gn, by_query)

    def memory_terms(core, dst):
        @pl.loop(0, NY)
        def _(i):
            cols = pl.ds(pl.multiple_of((i * 2 + core) * 512, 512), 512)
            term = lax.dot_general(S.gk[...], S.wk[cols, :], NT_DIMS, preferred_element_type=F32)
            term += lax.dot_general(S.gv[...], S.wv[cols, :], NT_DIMS, preferred_element_type=F32)
            dst[i] = term.astype(BF)

    def memory_other():
        memory_terms(other, S.msib_out)
        ring_m.send()

    def memory_own():
        memory_terms(c, S.mt)

    def grad_context():
        gather_0.done()
        gather_1.done()
        need(arriving.wo)

        @pl.loop(0, 2)
        def _(i):
            total = None
            for j in range(2):
                rows = call[j, pl.ds(i * 4, 4)].reshape(256, 2048)
                cols = S.wo[:, j * 2048 : j * 2048 + 2048]
                term = lax.dot_general(rows, cols, NT_DIMS, preferred_element_type=F32)
                total = term if total is None else total + term
            S.gctx[pl.ds(pl.multiple_of(i * 256, 256), 256), :] = total.astype(BF)

    def grad_values():
        grad_v = jnp.dot(S.p[...].T.astype(BF), S.gctx[...], preferred_element_type=F32)
        S.gv[...] = grad_v.astype(BF)
        S.gv_t[...] = grad_v.T.astype(BF)

    def backward():
        probs = S.p[...]
        grad_p = lax.dot_general(S.gctx[...], S.v[...], NT_DIMS, preferred_element_type=F32)
        grad_s = probs * (grad_p - jnp.sum(probs * grad_p, axis=1, keepdims=True)) * (HD**-0.5)
        grad_q = jnp.dot(grad_s.astype(BF), S.k[...], preferred_element_type=F32)
        S.gq[...] = grad_q.astype(BF).reshape(8, 64, HD)
        S.gq_t[...] = grad_q.T.astype(BF)
        grad_k = jnp.dot(grad_s.T.astype(BF), S.q[...], preferred_element_type=F32)
        S.gk[...] = grad_k.astype(BF)
        S.gk_t[...] = grad_k.T.astype(BF)

    def context_first():
        gather_0.done()

        @pl.loop(0, 4)
        def _(i):
            to.tile(early * 2 + i // 2, lax.rem(i, 2))

        to.xf.start_far()

    def context_last():
        gather_1.done()

        @pl.loop(0, 4)
        def _(i):
            to.tile((1 - early) * 2 + i // 2, lax.rem(i, 2))

        to.xf.start_near()
        to.zf.start()

    def layer_result():
        ring_a.ring.arrive(2)

        @pl.loop(0, 4)
        def _(i):
            rows = pl.ds(pl.multiple_of(i * 16, 16), 16)
            S.r_layer[i] = (S.shifted[rows, :] + ring_a.ring.total(rows)).astype(BF)

        results.r_layer.start()

    def decoder_result():
        S.part[...] = jnp.zeros_like(S.part)
        ring_g.ring.arrive(2)

        @pl.loop(0, 4)
        def _(i):
            rows = pl.ds(pl.multiple_of(i * 16, 16), 16)
            grad = ring_g.ring.total(rows)
            inv = S.inv[rows, 0:1]
            normed = S.shifted[rows, :] * inv
            product = grad * normed
            wide_gain = S.gain[...]
            dot_mean = jnp.mean(wide_gain * product, axis=1, keepdims=True)
            masked = jnp.concatenate([call[j, tp, rows] for j in range(2)], axis=1)
            shift = masked.astype(F32) + inv * (wide_gain * grad - normed * dot_mean)
            S.r_dec[i] = shift.astype(BF)
            S.part[3] += product[0:8] + product[8:16]
            both = shift[0:8] + shift[8:16]
            kind = jnp.full((8, D), objective[i], jnp.int32)
            for j in range(3):
                S.part[j] += jnp.where(kind == j, both, 0.0)

        results.r_dec.start()
        for i in range(4):
            total = jnp.sum(S.part[i], axis=0, keepdims=True)
            for t in range(8):
                S.s_out[t, i : i + 1, :] = total[:, t * 512 : t * 512 + 256]
                S.s_out[t, i + 4 : i + 5, :] = total[:, t * 512 + 256 : t * 512 + 512]
        S.s_in[tp] = S.s_out[tp]
        waits.s = exchange(S.s_out, S.s_in, NT, tp, lambda i: (dp, i), lambda i: i)

    def sum_x():
        waits.s()
        S.s_x[x] = jnp.sum(S.s_in[...], axis=0)
        waits.x = exchange(S.s_x, S.s_x, NX, x, lambda i: (i * NZ + z, tp), lambda i: x)

    def sum_z():
        waits.x()
        S.s_z[z] = jnp.sum(S.s_x[...], axis=0)
        waits.z = exchange(S.s_z, S.s_z, NZ, z, lambda i: (x * NZ + i, tp), lambda i: z)

    def sum_t():
        waits.z()
        S.s_all[tp] = jnp.sum(S.s_z[...], axis=0)
        waits.t = exchange(S.s_all, S.s_all, NT, tp, lambda i: (dp, i), lambda i: tp)

    def small_results():
        waits.t()
        for t in range(8):
            S.r_mode[:, t * 512 : t * 512 + 256] = S.s_all[t, 0:3, :]
            S.r_mode[:, t * 512 + 256 : t * 512 + 512] = S.s_all[t, 4:7, :]
            for i in range(4):
                at, low = (i % 2) * 128, 3 + i // 2 * 4
                S.r_gain[t * 4 + i : t * 4 + i + 1, :] = S.s_all[t, low : low + 1, at : at + 128]
        results.r_mode.start()
        results.r_gain.start()

    def send_back():
        ring_m.ring.arrive(2)
        S.b_out[...] = pack(1, ring_m.ring.total(pl.ds(0, 128)).astype(BF))
        S.b_in[dp] = S.b_out[dp]
        waits.b = exchange(S.b_out, S.b_in, NDP, dp, lambda i: (i, tp), lambda i: i)

    def memory_result():
        waits.b()
        back = unpack(0, S.b_in[...].reshape(512, 128))
        for j in range(4):
            S.back[:, j, :] = back[j * 32 : j * 32 + 32]
        S.r_mem[...] = S.back[...].astype(BF)
        results.r_mem.start()

    gather_n.own()
    send_examples()
    place_examples()
    gather_m.own()
    gather_n.forward()
    mask_cotangent()
    gather_m.middle()
    gather_m.forward()
    gather_0.own()
    gather_0.forward()
    gather_n.middle()
    gather_m.far()
    gather_n.far()
    gather_1.own()
    gather_0.middle()
    queries()
    keys_values()
    attention()
    gather_0.far()
    output_other()
    gather_1.forward()
    context_first()
    output_own()
    gather_1.middle()
    gather_1.far()
    output_ring()
    context_last()
    grad_context()
    backward()
    tk.first()
    to.zf.step(1)
    tk.near()
    tk.own()
    to.xf.step(1)
    normed_other()
    grad_values()
    to.zf.step(2)
    tq.first()
    tq.near()
    tk.zf.step(1)
    tq.own()
    normed_own()
    to.zf.step(3)
    ring_g.start()
    tk.xf.step(1)
    tv.first()
    tv.near()
    tv.own()
    tq.zf.step(1)
    tk.zf.step(2)
    memory_other()
    to.to_z()
    tv.zf.step(1)
    tq.zf.step(2)
    ring_g.ring.step(1)
    tk.to_z()
    to.xs.step(1)
    tv.zf.step(2)
    tq.xf.step(1)
    ring_a.ring.step(1)
    tk.xs.step(1)
    tk.zf.step(3)
    tq.zf.step(3)
    tv.xf.step(1)
    tk.xs.step(2)
    decoder_result()
    tv.zf.step(3)
    memory_own()
    tq.to_z()
    to.to_x()
    tk.to_x()
    ring_m.start()
    to.xs.step(2)
    tk.xs.step(3)
    sum_x()
    tv.to_z()
    tq.to_x()
    layer_result()
    ring_m.ring.step(1)
    tq.xs.step(1)
    tv.to_x()
    to.xs.step(3)
    tk.zs.step(1)
    tv.xs.step(1)
    tq.zs.step(1)
    sum_z()
    tq.xs.step(2)
    tv.xs.step(2)
    send_back()
    to.zs.step(1)
    tv.zs.step(1)
    tk.result(results.r_k)
    sum_t()
    tv.xs.step(3)
    tq.xs.step(3)
    small_results()
    to.result(results.r_o)
    memory_result()
    tv.result(results.r_v)
    tq.result(results.r_q)

    links.finish_sends()
    for one in vars(results).values():
        one.wait()


def place(*refs):
    count = len(RESULTS)
    held, sems = refs[2 * count : 3 * count], refs[3 * count]
    into = [pltpu.make_async_copy(refs[i], held[i], sems.at[0, i]) for i in range(count)]
    out = [pltpu.make_async_copy(held[i], refs[count + i], sems.at[1, i]) for i in range(count)]
    for one in into:
        one.start()
    for one, then in zip(into, out):
        one.wait()
        then.start()
    for one in out:
        one.wait()


def shards(
    decoder_states,
    encoder_memory,
    memory_route,
    memory_length,
    target_length,
    objective,
    mode_table,
    norm_gain,
    w_query,
    w_key,
    w_value,
    w_output,
    cotangent,
):
    smem = pl.BlockSpec(memory_space=pltpu.SMEM)
    hbm = pl.BlockSpec(memory_space=pl.ANY)
    out_shape = [jax.ShapeDtypeStruct(*one) for one in RESULTS.values()]
    found = pl.pallas_call(
        kernel,
        out_shape=out_shape,
        in_specs=[smem] * 2 + [hbm] * len(SOURCES),
        out_specs=[hbm] * len(RESULTS),
        scratch_shapes=[pltpu.VMEM(*one) for one in FLAT]
        + [
            pltpu.SemaphoreType.DMA((NSEND,)),
            pltpu.SemaphoreType.DMA((NRECV,)),
            pltpu.SemaphoreType.DMA((len(SOURCES) + len(RESULTS),)),
            pltpu.SemaphoreType.REGULAR,
        ],
        compiler_params=pltpu.CompilerParams(
            collective_id=0, has_side_effects=True, vmem_limit_bytes=62 * 1024 * 1024
        ),
        cost_estimate=pl.CostEstimate(flops=8 * 10**9, bytes_accessed=12 * 10**6, transcendentals=10**5),
    )(
        target_length,
        objective,
        mode_table,
        norm_gain.reshape(32, 128),
        decoder_states,
        memory_route.reshape(8, 128),
        memory_length.reshape(8, 128),
        encoder_memory,
        cotangent,
        w_query,
        w_key,
        w_value,
        w_output,
    )
    layer, dec, mem, gq, gk, gv, go, gain, mode = pl.pallas_call(
        place,
        out_shape=out_shape,
        in_specs=[hbm] * len(RESULTS),
        out_specs=[hbm] * len(RESULTS),
        scratch_shapes=[pltpu.VMEM(*one) for one in RESULTS.values()]
        + [pltpu.SemaphoreType.DMA((2, len(RESULTS)))],
    )(*found)
    return layer, dec, mem, gq, gk, gv, go, gain.reshape(D), mode


def solution(mesh):
    return jax.shard_map(
        shards,
        mesh=mesh,
        in_specs=(
            P(("dp", "tensor"), None, None),
            P("dp", None, "tensor"),
            P(),
            P(),
            P(("dp", "tensor")),
            P(("dp", "tensor")),
            P(),
            P(),
            P(None, "tensor"),
            P(None, "tensor"),
            P(None, "tensor"),
            P("tensor", None),
            P(("dp", "tensor"), None, None),
        ),
        out_specs=(
            P(("dp", "tensor"), None, None),
            P(("dp", "tensor"), None, None),
            P("dp", None, "tensor"),
            P("dp", "tensor"),
            P("dp", "tensor"),
            P("dp", "tensor"),
            P("tensor", "dp"),
            P(),
            P(),
        ),
        check_vma=False,
    )
```

time: 1400 us -> 113 us (0.08)
  waiting for transfers between devices: 1270 us -> 0 us
  Pallas kernels: 0 us -> 112 us
  matrix products: 45.6 us -> 0 us
  starting transfers between devices: 22.1 us -> 0 us
  local copies, waits for them, and re-layouts: 21 us -> 0 us
  other arithmetic: 19.6 us -> 0 us
    reduce_scatter x6 -> x0, waiting for transfers between devices: 722 us -> none  [the longest x1 219 us: shards(): lax.psum_scatter(weight_terms[2].astype(jnp.bfloat16), 'dp', scatter_dime...]
    psum x1 -> x0, waiting for transfers between devices: 251 us -> none  [shards(): grad_gain, grad_mode = lax.psum((gain_term, mode_term), ('dp', 'tensor'))]
    unnamed x12 -> x0, waiting for transfers between devices: 211 us -> none
    pallas_call x0 -> x2, Pallas kernels: none -> 112 us  [the longest x1 110 us: shards(): pl.pallas_call(kernel, out_shape=out_shape, in_specs=[smem] * 2 + [hbm] *...]
    all_gather x3 -> x0, waiting for transfers between devices: 85.7 us -> none  [the longest x1 33.7 us: shards(): all_normed = lax.all_gather(normed_in, 'tensor', axis=0, tiled=True)]
    dot_general x20 -> x0, matrix products: 45.6 us -> none  [the longest x1 4.85 us: shards(): jnp.einsum('btd,wd->btw', all_cot, w_output, preferred_element_type=jnp.f...]
    all_to_all x2 -> x0, starting transfers between devices: 21.4 us -> none  [the longest x1 11.9 us: shards(): lax.all_to_all(send_rows, 'dp', split_axis=0, concat_axis=0, tiled=True)]
  transfers between devices with their start and end apart: 13 -> 0, of which waited for: 11 -> 0; matrix products, arithmetic and copies ran while one was open for 4% -> 0% of each run, Pallas kernels for 0% -> 0%
where the time goes in v2:
time: 113 us
  Pallas kernels  112 us (99%)
    pallas_call x1, Pallas kernels, shards(): pl.pallas_call(kernel, out_shape=out_shape, in_specs=[smem] * 2 + [hbm] *...  110 us
    pallas_call x1, Pallas kernels, shards(): pl.pallas_call(place, out_shape=out_shape, in_specs=[hbm] * len(RESULTS),...  2.32 us

profile of v2, /device:TPU:1, one launch (start us, length us, event | category | flops | bytes accessed | tf_op | source)
XLA Modules:
  0.0 113.1 jit_solution(15593642461762946141)
XLA Ops:
  0.6 110.2 %shard_map.196 = (bf16[4,16,4096]{2,1,0:T(8,128)(2,1)}, bf16[4,16,4096]{2,1,0:T(8,128)(2,1)}, bf16[32,4,512]{2,1,0:T(4,128)(2,1)}, bf16[128,256]{1,0:T(8,128)(2,...) custom-call(s32[4]{0:T(128)} %refs_0_.1, ...), custom_call_target="tpu_custom_call" | custom-call | flops 8000000000 | bytes 12000000 | tf_op jit(solution)/shard_map/pallas_call | solution.py:888
  110.8 2.3 %shard_map.197 = (bf16[4,16,4096]{2,1,0:T(8,128)(2,1)}, bf16[4,16,4096]{2,1,0:T(8,128)(2,1)}, bf16[32,4,512]{2,1,0:T(4,128)(2,1)}, bf16[128,256]{1,0:T(8,128)(2,...) custom-call(bf16[4,16,4096]{2,1,0:T(8,128)(2,1)} %get-tuple-element., ...), custom_call_target="tpu_custom_call" | custom-call | tf_op jit(solution)/shard_map/pallas_call | solution.py:919
